TPU v7x, 32 devices: a whole 2x2x4 slice. The times are simulated.
32 devices in a mesh: groups: 2 (over y), expert: 4 (over z), tensor: 4 (over x, core).
Axes of the slice: x: 2, y: 2, z: 4, core: 2. Of those that a mesh axis runs over, the one named last changes fastest.
Arguments:
- resid: bfloat16 [256, 3072], P(('groups', 'expert', 'tensor')), parts along dimension 0, may hold values from -6 to 6
- attn_part: bfloat16 [256, 12288], P(('groups', 'expert'), 'tensor'), parts along dimension 0, may hold values from -2 to 2
- norm_gain: float32 [3072], replicated, may hold values from 0.1 to 1.9
- w_router: bfloat16 [3072, 8], replicated, may hold values from -0.3125 to 0.3125
- routes: int32 [256, 2], P(('groups', 'expert', 'tensor')), parts along dimension 0, may hold values from 0 to 7, all different within a row; in each aligned block of 8 rows (0 to 7, 8 to 15, ...) at most 4 rows name the same one
- w_gate: bfloat16 [3072, 65536], P(None, ('expert', 'tensor')), may hold values from -0.109375 to 0.109375
- w_up: bfloat16 [3072, 65536], P(None, ('expert', 'tensor')), may hold values from -0.109375 to 0.109375
- w_down: bfloat16 [65536, 3072], P(('expert', 'tensor')), may hold values from -0.0625 to 0.0625
Outputs:
- block_out: bfloat16 [256, 3072], P(('groups', 'expert', 'tensor')), parts along dimension 0
There are 2 independent parts, one for each index of `groups`. A program takes and returns all parts, laid end to end along the dimension named above; an argument that names none is the same for every part. Nothing has to cross between parts.
Inputs may be any that keep to these rules, and one draw needn't show every extreme that they name: `routes`: the two entries of a row differ. Within the 8 rows of one device no expert is named more than 4 times, and in some device's rows some expert is named exactly 4 times.
All inputs are finite; a program needn't handle non-finite values.
Results may differ from a plain program's by a relative error of at most 0.02.
Values may be sent and summed in bfloat16 or wider, within the bound.
A program may use at most 128 MiB of HBM per device.

v0:
```python
import jax
import jax.numpy as jnp
from jax import lax
from jax.sharding import PartitionSpec as P

E = 8


EPSILON = 1e-05


def partner(shard, axis, distance):
    return lax.ppermute(shard, axis, [(i, i ^ 1 << distance) for i in range(lax.axis_size(axis))])


def shards(resid, attn_part, norm_gain, w_router, routes, w_gate, w_up, w_down):
    expert_ranks = lax.axis_size("expert")
    tensor_ranks = lax.axis_size("tensor")
    my_expert_rank = lax.axis_index("expert")
    my_tensor_rank = lax.axis_index("tensor")
    token_rows = resid.shape[0]
    feature_count = resid.shape[1]
    holders = max(1, expert_ranks // E)
    hosted = max(1, E // expert_ranks)
    expert_groups = E // hosted
    capacity = token_rows // 2
    rank_slots = hosted * capacity
    feature_share = feature_count // holders
    levels = holders.bit_length() - 1
    partial_terms = attn_part.astype(jnp.float32)
    attn_rows = lax.psum_scatter(
        partial_terms.astype(jnp.bfloat16), "tensor", scatter_dimension=0, tiled=True
    ).astype(jnp.float32)
    hidden_state = (resid.astype(jnp.float32) + attn_rows).astype(jnp.bfloat16)
    hidden_wide = lax.optimization_barrier(hidden_state).astype(jnp.float32)
    inverse_rms = lax.rsqrt(jnp.mean(hidden_wide * hidden_wide, axis=1, keepdims=True) + EPSILON)
    normed = (hidden_wide * inverse_rms * norm_gain).astype(jnp.bfloat16)
    logits = jnp.dot(normed, w_router, preferred_element_type=jnp.float32)
    expert_columns = lax.broadcasted_iota(jnp.int32, (token_rows, E), 1)
    pick_first = (routes[:, 0:1] == expert_columns).astype(jnp.float32)
    pick_second = (routes[:, 1:2] == expert_columns).astype(jnp.float32)
    share_first = jax.nn.sigmoid(jnp.sum((pick_first - pick_second) * logits, axis=1))
    share_second = 1.0 - share_first
    row_later = lax.broadcasted_iota(jnp.int32, (token_rows, token_rows), 0)
    row_earlier = lax.broadcasted_iota(jnp.int32, (token_rows, token_rows), 1)
    earlier = (row_later > row_earlier).astype(jnp.float32)
    before = jnp.dot(earlier, pick_first + pick_second, precision=lax.Precision.HIGHEST)
    slot_first = jnp.sum(before * pick_first, axis=1)
    slot_second = jnp.sum(before * pick_second, axis=1)
    slot_numbers = lax.broadcasted_iota(jnp.int32, (token_rows, E, capacity), 2).astype(jnp.float32)
    cell_first = pick_first[:, :, None] * (slot_numbers == slot_first[:, None, None]).astype(
        jnp.float32
    )
    cell_second = pick_second[:, :, None] * (slot_numbers == slot_second[:, None, None]).astype(
        jnp.float32
    )
    placement = (
        (cell_first + cell_second)
        .reshape(token_rows, expert_groups, rank_slots)
        .astype(jnp.bfloat16)
    )
    combine_weight = (
        share_first[:, None, None] * cell_first + share_second[:, None, None] * cell_second
    ).reshape(token_rows, expert_groups, rank_slots)
    outgoing = jnp.einsum(
        "rgc,rd->gcd", placement, normed, preferred_element_type=jnp.float32
    ).astype(jnp.bfloat16)
    outgoing = jnp.repeat(outgoing, holders, axis=0)
    arrived = lax.all_to_all(outgoing, "expert", split_axis=0, concat_axis=0, tiled=True)
    device_span = my_expert_rank * tensor_ranks + my_tensor_rank
    own_expert = device_span * E // (expert_ranks * tensor_ranks)
    local_index = own_expert - my_expert_rank // holders * hosted

    def activate(token_block):
        source_count = token_block.shape[0]
        selected = lax.dynamic_slice_in_dim(token_block, local_index * capacity, capacity, 1)
        flattened = selected.reshape(source_count * capacity, feature_count)
        gate_value = jnp.dot(flattened, w_gate, preferred_element_type=jnp.float32)
        up_value = jnp.dot(flattened, w_up, preferred_element_type=jnp.float32)
        return (jax.nn.silu(gate_value) * up_value).astype(jnp.bfloat16)

    def expert_partial(token_block):
        source_count = token_block.shape[0]
        activated = activate(token_block)
        produced = jnp.dot(activated, w_down, preferred_element_type=jnp.float32).reshape(
            source_count, capacity, feature_count
        )
        if hosted == 1:
            return produced
        blank = jnp.zeros((source_count, rank_slots, feature_count), jnp.float32)
        return lax.dynamic_update_slice_in_dim(blank, produced, local_index * capacity, 1)

    partial_value = expert_partial(lax.all_gather(arrived, "tensor", axis=0, tiled=True))
    leading = partial_value.shape[0]
    layered = partial_value.reshape((leading, rank_slots) + (2,) * levels + (feature_share,))
    remaining = [section for section in range(levels - 1, -1, -1)]
    for section in range(levels):
        split_axis = 2 + remaining.index(section)
        my_side = my_expert_rank // 2**section % 2
        kept_half = lax.dynamic_index_in_dim(layered, my_side, split_axis, keepdims=False)
        given_half = lax.dynamic_index_in_dim(layered, 1 - my_side, split_axis, keepdims=False)
        layered = kept_half + partner(given_half.astype(jnp.bfloat16), "expert", section).astype(
            given_half.dtype
        )
        remaining = [other for other in remaining if other != section]
    own_sources = lax.psum_scatter(
        layered.astype(jnp.bfloat16), "tensor", scatter_dimension=0, tiled=True
    ).astype(jnp.float32)
    returned = lax.all_to_all(
        own_sources.astype(jnp.bfloat16), "expert", split_axis=0, concat_axis=0, tiled=True
    ).astype(own_sources.dtype)
    returned_view = returned.reshape(expert_groups, holders, rank_slots, feature_share)
    mixed = jnp.einsum(
        "rgc,gscp->rsp", combine_weight, returned_view, precision=lax.Precision.HIGHEST
    )
    mixed = mixed.reshape(token_rows, feature_count)
    return (hidden_wide + mixed).astype(jnp.bfloat16)


def solution(mesh):
    return jax.shard_map(
        shards,
        mesh=mesh,
        in_specs=(
            P(("groups", "expert", "tensor"), None),
            P(("groups", "expert"), "tensor"),
            P(),
            P(),
            P(("groups", "expert", "tensor"), None),
            P(None, ("expert", "tensor")),
            P(None, ("expert", "tensor")),
            P(("expert", "tensor"), None),
        ),
        out_specs=P(("groups", "expert", "tensor"), None),
        check_vma=False,
    )
```

profile of v0, /device:TPU:0, one launch (start us, length us, event | category | flops | bytes accessed | tf_op | source)
XLA Modules:
  0.0 129.9 jit_solution(15050298465613844478)
XLA Ops:
  6.5 0.0 copy-start
  6.5 0.0 reduce-scatter.3.cloned.1.call-start
  6.5 0.7 reduce-scatter.3.cloned.1.call-update
  7.3 0.8 slice_bitcast_fusion.1
  8.0 0.1 iota.42
  8.1 0.1 select_reduce_fusion.1
  8.3 24.0 %reduce-scatter.3.cloned.1.call-done = bf16[8,3072]{1,0:T(8,128)(2,1)} async-done(((bf16[32,3072]{1,0:T(8,128)(2,1)}), bf16[8,3072]{1,0:T(8,128)(2,1)}) %reduce-scatter.3.cloned.1.call-update) | async-done | bytes 49168 | tf_op jit(solution)/shard_map/reduce_scatter | solution.py:31
  32.3 0.8 add_convert_fusion
  33.1 0.1 fusion.11
  33.3 0.0 copy-done
  33.3 0.9 fusion.4
  34.2 0.1 fusion.18
  34.3 1.6 %convolution_convert_fusion = bf16[4,8,3072]{2,1,0:T(8,128)(2,1)} fusion(bf16[8,4,8]{0,2,1:T(8,128)(2,1)S(1)} %get-tuple-element.9, bf16[8,3072]{1,0:T(8,128)(2,1)S(1)} %add_convert_fusion, f32[3072]{0:T(1024)} %param.10, f32[8]{0:T(128)S(1)} %add_rsqrt_fusion), kind=kOutput, calls=%fused_computation.2 | convolution fusion | flops 1769472 | bytes 258592 | tf_op jit(solution)/shard_map/rgc,rd->gcd/dot_general | solution.py:65
  35.9 4.6 %all-to-all-start = ((bf16[4,8,3072]{2,1,0:T(8,128)(2,1)}), bf16[4,8,3072]{2,1,0:T(8,128)(2,1)S(1)}, u32[]{:S(2)}, u32[]{:S(2)}) async-start(bf16[4,8,3072]{2,1,0:T(8,128)(2,1)} %convolution_convert_fusion), calls=%async_computation.1 | async-start | bytes 393216 | tf_op jit(solution)/shard_map/all_to_all | solution.py:69
  40.5 0.0 reduce-scatter.5.cloned.1.call-start
  40.5 7.3 %all-to-all-done = bf16[4,8,3072]{2,1,0:T(8,128)(2,1)S(1)} async-done(((bf16[4,8,3072]{2,1,0:T(8,128)(2,1)}), bf16[4,8,3072]{2,1,0:T(8,128)(2,1)S(1)}, u32[]{:S(2)}, u32[]{:S(2)}) %all-to-all-start) | async-done | bytes 196640 | tf_op jit(solution)/shard_map/all_to_all | solution.py:69
  47.8 7.7 %all_gather.3 = bf16[16,8,3072]{2,1,0:T(8,128)(2,1)S(1)} all-gather(bf16[4,8,3072]{2,1,0:T(8,128)(2,1)S(1)} %all-to-all-done), channel_id=1, replica_groups=mesh['groups'=2,'expert'=4,'tensor'=4] {'tensor'}, dimensions={0}, use_global_device_ids=true | all-gather | bytes 983040 | tf_op jit(solution)/shard_map/all_gather | solution.py:93
  55.5 0.2 constant_dynamic-slice_fusion
  55.7 0.1 reshape.88
  55.8 10.5 %fusion.31 = f32[64,4096]{1,0:T(8,128)S(1)} fusion(bf16[64,3072]{1,0:T(8,128)(2,1)S(1)} %reshape.88, bf16[3072,4096]{1,0:T(8,128)(2,1)} %param.13), kind=kOutput, calls=%fused_computation.49 | convolution fusion | flops 1610612736 | bytes 26607616 | tf_op jit(solution)/shard_map/dot_general | solution.py:78
  66.3 19.9 %fusion.3 = bf16[64,3072]{1,0:T(8,128)(2,1)S(1)} fusion(bf16[4096,3072]{1,0:T(8,128)(2,1)} %param.15, bf16[64,3072]{1,0:T(8,128)(2,1)S(1)} %reshape.88, bf16[3072,4096]{1,0:T(8,128)(2,1)} %param.14, f32[64,4096]{1,0:T(8,128)S(1)} %fusion.31), kind=kOutput, calls=%fused_computation.6 | convolution fusion | flops 3222798336 | bytes 52166656 | tf_op jit(solution)/shard_map/dot_general | solution.py:85
  86.2 0.1 reshape.89
  86.3 0.1 broadcast_in_dim.2
  86.4 0.3 constant_dynamic-update-slice_fusion
  86.7 0.0 copy-start.1
  86.7 0.9 copy-done.1
  87.6 0.0 reduce-scatter.5.cloned.1.call-update
  87.6 22.5 %reduce-scatter.5.cloned.1.call-done = bf16[4,8,3072]{2,1,0:T(8,128)(2,1)} async-done(((bf16[16,8,3072]{2,1,0:T(8,128)(2,1)}), bf16[4,8,3072]{2,1,0:T(8,128)(2,1)}) %reduce-scatter.5.cloned.1.call-update) | async-done | bytes 196624 | tf_op jit(solution)/shard_map/reduce_scatter | solution.py:106
  110.1 12.1 %all_to_all.10 = bf16[4,8,3072]{2,1,0:T(8,128)(2,1)S(1)} all-to-all(bf16[4,8,3072]{2,1,0:T(8,128)(2,1)} %reduce-scatter.5.cloned.1.call-done), channel_id=1, replica_groups=mesh['groups'=2,'expert'=4,'tensor'=4] {'expert'}, dimensions={0} | all-to-all | bytes 393216 | tf_op jit(solution)/shard_map/all_to_all | solution.py:109
  122.2 0.9 fusion.2
  (7 shorter events, 0.0 us)
Async XLA Ops:
  6.5 26.7 %copy-start = (bf16[3072,8]{0,1:T(8,128)(2,1)S(1)}, bf16[3072,8]{0,1:T(8,128)(2,1)}, u32[]{:S(2)}) copy-start(bf16[3072,8]{0,1:T(8,128)(2,1)} %param.11) | copy-start | bytes 147460
  6.5 25.7 %reduce-scatter.3.cloned.1.call-start = ((), (), s32[]{:S(2)}) async-start(), calls=%async_computation.4 | async-start | bytes 245760 | tf_op jit(solution)/shard_map/reduce_scatter | solution.py:31
  35.9 11.9 %all-to-all-start = ((bf16[4,8,3072]{2,1,0:T(8,128)(2,1)}), bf16[4,8,3072]{2,1,0:T(8,128)(2,1)S(1)}, u32[]{:S(2)}, u32[]{:S(2)}) async-start(bf16[4,8,3072]{2,1,0:T(8,128)(2,1)} %convolution_convert_fusion), calls=%async_computation.1 | async-start | bytes 393216 | tf_op jit(solution)/shard_map/all_to_all | solution.py:69
  40.5 69.6 %reduce-scatter.5.cloned.1.call-start = ((), (), s32[]{:S(2)}) async-start(), calls=%async_computation.5 | async-start | bytes 983040 | tf_op jit(solution)/shard_map/reduce_scatter | solution.py:106
  86.7 0.9 copy-start.1
Sparse Core Ops, SparseCore 0:
  9.8 22.4 reduce-scatter.2
  87.7 22.3 reduce-scatter.4
where the time goes:
time: 130 us
  waiting for transfers between devices  54.6 us (42%)
  matrix products  33.9 us (26%)
  blocking collectives  19.7 us (15%)
  between operations  13.5 us (10%)
  starting transfers between devices  4.58 us (4%)
  local copies, waits for them, and re-layouts  2.53 us (2%)
    reduce_scatter x1, waiting for transfers between devices, shards(): lax.psum_scatter(partial_terms.astype(jnp.bfloat16), 'tensor', scatter_di...  24 us
    reduce_scatter x1, waiting for transfers between devices, shards(): lax.psum_scatter(layered.astype(jnp.bfloat16), 'tensor', scatter_dimensio...  22.5 us
    dot_general x1, matrix products, expert_partial(): jnp.dot(activated, w_down, preferred_element_type=jnp.float32)  19.9 us
    all_to_all x1, blocking collectives, shards(): lax.all_to_all(own_sources.astype(jnp.bfloat16), 'expert', split_axis=0,...  12.1 us
    dot_general x1, matrix products, activate(): gate_value = jnp.dot(flattened, w_gate, preferred_element_type=jnp.float32)  10.5 us
    all_gather x1, blocking collectives, shards(): lax.all_gather(arrived, 'tensor', axis=0, tiled=True)  7.66 us
    all_to_all x1, waiting for transfers between devices, shards(): lax.all_to_all(outgoing, 'expert', split_axis=0, concat_axis=0, tiled=True)  7.33 us
    all_to_all x1, starting transfers between devices, shards(): lax.all_to_all(outgoing, 'expert', split_axis=0, concat_axis=0, tiled=True)  4.58 us
  transfers between devices with their start and end apart: 3, of which 3 were waited for; matrix products, arithmetic and copies ran while one was open for 1% of the time, Pallas kernels for 0%

commit v1 on v0

--- a/solution.py
+++ b/solution.py
@@ -1,9 +1,14 @@
+import functools
+
 import jax
 import jax.numpy as jnp
 from jax import lax
+from jax.experimental import pallas as pl
+from jax.experimental.pallas import tpu as pltpu
 from jax.sharding import PartitionSpec as P
 
 E = 8
+MESH = pl.DeviceIdType.MESH
 
 
 EPSILON = 1e-05
@@ -117,9 +122,431 @@
     return (hidden_wide + mixed).astype(jnp.bfloat16)
 
 
+LANES = 128
+PACKED_ROWS = 16
+WEIGHT_BYTES = 52 << 20
+VMEM_BYTES = 60 << 20
+
+
+def fused_kernel(
+    sizes,
+    resid_hbm,
+    attn_hbm,
+    gain_hbm,
+    router_hbm,
+    routes_hbm,
+    gate_hbm,
+    up_hbm,
+    down_hbm,
+    out_ref,
+    resid,
+    attn,
+    gain,
+    router,
+    routes,
+    in_sem,
+    hidden_weights,
+    hidden_sem,
+    down_weights,
+    down_sem,
+    attn_out,
+    attn_in,
+    attn_out_sem,
+    attn_in_sem,
+    hidden_ref,
+    share_ref,
+    slots_out,
+    slots_in,
+    slots_out_sem,
+    slots_in_sem,
+    pass_out_sem,
+    pass_in_sem,
+    tokens,
+    activated,
+    partial_ref,
+    half_out,
+    half_in,
+    half_out_sem,
+    half_in_sem,
+    back_out,
+    back_in,
+    back_out_sem,
+    back_in_sem,
+):
+    experts, tensor_ranks, capacity, hidden_slots, down_slots = sizes
+    rows, features = resid.shape
+    fold = PACKED_ROWS // capacity
+    width = features // fold
+    hidden_step = hidden_weights.shape[3]
+    hidden_steps = gate_hbm.shape[1] // hidden_step
+    down_step = down_weights.shape[2]
+    down_steps = features // down_step
+    pairs = tensor_ranks // 2
+    group = lax.axis_index("groups")
+    my_z = lax.axis_index("expert")
+    my_t = lax.axis_index("tensor")
+    core = my_t % 2
+    me = my_z * pairs + my_t // 2
+    sibling = (group, my_z, my_t + 1 - 2 * core)
+
+    def holder(number):
+        return (group, number // pairs, (number % pairs) * 2 + core)
+
+    def after(step):
+        return (me + step) % experts
+
+    def before(step):
+        return (me + experts - step) % experts
+
+    small = [
+        pltpu.make_async_copy(source, target, in_sem.at[i])
+        for i, (source, target) in enumerate(
+            (
+                (attn_hbm, attn),
+                (resid_hbm, resid),
+                (gain_hbm, gain),
+                (router_hbm, router),
+                (routes_hbm, routes),
+            )
+        )
+    ]
+    for copy in small:
+        copy.start()
+
+    def hidden_copies(step, slot):
+        columns = pl.ds(pl.multiple_of(step * hidden_step, hidden_step), hidden_step)
+        return [
+            pltpu.make_async_copy(
+                source.at[:, columns], hidden_weights.at[slot, i], hidden_sem.at[slot, i]
+            )
+            for i, source in enumerate((gate_hbm, up_hbm))
+        ]
+
+    def down_copy(step, slot):
+        columns = pl.ds(pl.multiple_of(step * down_step, down_step), down_step)
+        return pltpu.make_async_copy(
+            down_hbm.at[:, columns], down_weights.at[slot], down_sem.at[slot]
+        )
+
+    for step in range(hidden_slots):
+        for copy in hidden_copies(step, step):
+            copy.start()
+
+    barrier = pltpu.get_barrier_semaphore()
+    tensor_peers = [(group, my_z, (my_t + i) % tensor_ranks) for i in range(1, tensor_ranks)]
+    peers = [holder(after(i)) for i in range(1, experts)]
+    for peer in tensor_peers + peers:
+        pl.semaphore_signal(barrier, inc=1, device_id=peer, device_id_type=MESH)
+
+    small[0].wait()
+    terms = attn[...].astype(jnp.float32)
+    half = features // 2
+    for i in range(tensor_ranks):
+        block = terms[i * rows : (i + 1) * rows]
+        attn_out[i] = jnp.concatenate([block[:, :half], block[:, half:]], axis=0).astype(
+            jnp.bfloat16
+        )
+    pl.semaphore_wait(barrier, len(tensor_peers) + len(peers))
+
+    def attn_copy(step):
+        target = (my_t + step) % tensor_ranks
+        return pltpu.make_async_remote_copy(
+            src_ref=attn_out.at[target],
+            dst_ref=attn_in.at[step - 1],
+            send_sem=attn_out_sem.at[step - 1],
+            recv_sem=attn_in_sem.at[step - 1],
+            device_id=(group, my_z, target),
+            device_id_type=MESH,
+        )
+
+    attn_copies = [attn_copy(step) for step in range(1, tensor_ranks)]
+    for copy in attn_copies:
+        copy.start()
+    for copy in small[1:]:
+        copy.wait()
+    route = routes[...]
+    first, second = route[:, 0:1], route[:, 1:2]
+    columns = lax.broadcasted_iota(jnp.int32, (rows, LANES), 1)
+    row_number = lax.broadcasted_iota(jnp.int32, (rows, LANES), 0)
+    pick_first = (columns == first).astype(jnp.float32)
+    pick_second = (columns == second).astype(jnp.float32)
+    both = pick_first + pick_second
+    earlier = jnp.zeros((rows, LANES), jnp.float32)
+    for i in range(rows):
+        earlier += jnp.where(row_number > i, both[i : i + 1], 0.0)
+    slot_first = jnp.sum(earlier * pick_first, axis=1, keepdims=True).astype(jnp.int32)
+    slot_second = jnp.sum(earlier * pick_second, axis=1, keepdims=True).astype(jnp.int32)
+    place_first = jnp.concatenate([first * PACKED_ROWS + slot_first] * fold, axis=0)
+    place_second = jnp.concatenate([second * PACKED_ROWS + slot_second] * fold, axis=0)
+    packed = experts * PACKED_ROWS
+    part = lax.broadcasted_iota(jnp.int32, (fold * rows, packed), 0) // rows * capacity
+    cells = lax.broadcasted_iota(jnp.int32, (fold * rows, packed), 1) - part
+    cell_first = (cells == place_first).astype(jnp.float32)
+    cell_second = (cells == place_second).astype(jnp.float32)
+    placement = (cell_first + cell_second).T.astype(jnp.bfloat16)
+
+    summed = attn_out[my_t].astype(jnp.float32)
+    for i, copy in enumerate(attn_copies):
+        copy.wait_recv()
+        summed += attn_in[i].astype(jnp.float32)
+    attn_sum = jnp.concatenate([summed[:rows], summed[rows:]], axis=1)
+    hidden_wide = (
+        (resid[...].astype(jnp.float32) + attn_sum).astype(jnp.bfloat16).astype(jnp.float32)
+    )
+    hidden_ref[...] = hidden_wide
+    mean_square = jnp.sum(hidden_wide * hidden_wide, axis=1, keepdims=True) / features
+    normed_wide = hidden_wide * lax.rsqrt(mean_square + EPSILON) * gain[...]
+    normed = normed_wide.astype(jnp.bfloat16)
+    folded = jnp.concatenate(
+        [normed_wide[:, i * width : (i + 1) * width] for i in range(fold)], axis=0
+    ).astype(jnp.bfloat16)
+    outgoing = jnp.dot(placement, folded, preferred_element_type=jnp.float32)
+    slots_out[...] = outgoing.astype(jnp.bfloat16).reshape(experts, PACKED_ROWS, width)
+
+    def slot_copy(step):
+        return pltpu.make_async_remote_copy(
+            src_ref=slots_out.at[after(step)],
+            dst_ref=slots_in.at[core, me],
+            send_sem=slots_out_sem.at[step],
+            recv_sem=slots_in_sem.at[step],
+            device_id=holder(after(step)),
+            device_id_type=MESH,
+        )
+
+    def pass_copy(step):
+        source = slots_out.at[me] if step == 0 else slots_in.at[core, before(step)]
+        return pltpu.make_async_remote_copy(
+            src_ref=source,
+            dst_ref=slots_in.at[core, before(step)],
+            send_sem=pass_out_sem.at[step],
+            recv_sem=pass_in_sem.at[step],
+            device_id=sibling,
+            device_id_type=MESH,
+        )
+
+    slot_copies = [slot_copy(step) for step in range(1, experts)]
+    for copy in slot_copies:
+        copy.start()
+    pass_copies = [pass_copy(step) for step in range(experts)]
+    pass_copies[0].start()
+    for step in range(down_slots):
+        down_copy(step, step).start()
+    slots_in[core, me] = slots_out[me]
+
+    logits = jnp.dot(normed, router[...], preferred_element_type=jnp.float32)
+    expert_columns = lax.broadcasted_iota(jnp.int32, (rows, experts), 1)
+    logit_first = jnp.sum(jnp.where(expert_columns == first, logits, 0.0), axis=1, keepdims=True)
+    logit_second = jnp.sum(jnp.where(expert_columns == second, logits, 0.0), axis=1, keepdims=True)
+    share_first = 1.0 / (1.0 + jnp.exp(logit_second - logit_first))
+    share_second = 1.0 - share_first
+    share_ref[...] = (
+        jnp.concatenate([share_first] * fold, axis=0) * cell_first
+        + jnp.concatenate([share_second] * fold, axis=0) * cell_second
+    )
+
+    for step in range(1, experts):
+        slot_copies[step - 1].wait_recv()
+        pass_copies[step].start()
+    for copy in pass_copies:
+        copy.wait_recv()
+
+    sources = 2 * experts
+    token_rows = sources * capacity
+    arrived = slots_in[...].reshape(sources * PACKED_ROWS, width)
+    token_number = lax.broadcasted_iota(jnp.int32, (token_rows, sources * PACKED_ROWS), 0)
+    packed_number = lax.broadcasted_iota(jnp.int32, (token_rows, sources * PACKED_ROWS), 1)
+    wanted = token_number // capacity * PACKED_ROWS + token_number % capacity
+    for i in range(fold):
+        select = (packed_number == wanted + i * capacity).astype(jnp.float32).astype(jnp.bfloat16)
+        tokens[:, i * width : (i + 1) * width] = jnp.dot(
+            select, arrived, preferred_element_type=jnp.float32
+        ).astype(jnp.bfloat16)
+
+    def hidden_body(step, carry):
+        slot = step % hidden_slots
+        for copy in hidden_copies(step, slot):
+            copy.wait()
+        gate_value = jnp.dot(
+            tokens[...], hidden_weights[slot, 0], preferred_element_type=jnp.float32
+        )
+        up_value = jnp.dot(tokens[...], hidden_weights[slot, 1], preferred_element_type=jnp.float32)
+        value = gate_value / (1.0 + jnp.exp(-gate_value)) * up_value
+        activated[:, pl.ds(pl.multiple_of(step * hidden_step, hidden_step), hidden_step)] = (
+            value.astype(jnp.bfloat16)
+        )
+
+        @pl.when(step + hidden_slots < hidden_steps)
+        def _():
+            for copy in hidden_copies(step + hidden_slots, slot):
+                copy.start()
+
+        return carry
+
+    lax.fori_loop(0, hidden_steps, hidden_body, 0)
+
+    half_rows = experts * capacity
+
+    def half_copy(step):
+        return pltpu.make_async_remote_copy(
+            src_ref=half_out.at[step],
+            dst_ref=half_in.at[step],
+            send_sem=half_out_sem.at[step],
+            recv_sem=half_in_sem.at[step],
+            device_id=sibling,
+            device_id_type=MESH,
+        )
+
+    def back_copy(step, distance):
+        return pltpu.make_async_remote_copy(
+            src_ref=back_out.at[step, after(distance)],
+            dst_ref=back_in.at[step, me],
+            send_sem=back_out_sem.at[step, distance],
+            recv_sem=back_in_sem.at[step, distance],
+            device_id=holder(after(distance)),
+            device_id_type=MESH,
+        )
+
+    to_row = lax.broadcasted_iota(jnp.int32, (packed, packed), 0)
+    from_row = lax.broadcasted_iota(jnp.int32, (packed, packed), 1)
+    origin = (
+        to_row % PACKED_ROWS // capacity * half_rows
+        + to_row // PACKED_ROWS * capacity
+        + to_row % capacity
+    )
+    reorder = (from_row == origin).astype(jnp.float32).astype(jnp.bfloat16)
+
+    def send_back(step):
+        half_copy(step).wait_recv()
+        total = partial_ref[step, core] + half_in[step].astype(jnp.float32)
+        stacked = jnp.concatenate(
+            [total[:, i * LANES : (i + 1) * LANES] for i in range(fold)], axis=0
+        ).astype(jnp.bfloat16)
+        ordered = jnp.dot(reorder, stacked, preferred_element_type=jnp.float32)
+        back_out[step] = ordered.astype(jnp.bfloat16).reshape(experts, PACKED_ROWS, LANES)
+        for distance in range(1, experts):
+            back_copy(step, distance).start()
+        back_in[step, me] = back_out[step, me]
+
+    def down_body(step, carry):
+        slot = step % down_slots
+        down_copy(step, slot).wait()
+        produced = jnp.dot(activated[...], down_weights[slot], preferred_element_type=jnp.float32)
+        partial_ref[step] = produced.reshape(2, half_rows, down_step)
+
+        @pl.when(step + down_slots < down_steps)
+        def _():
+            down_copy(step + down_slots, slot).start()
+
+        half_out[step] = partial_ref[step, 1 - core].astype(jnp.bfloat16)
+        half_copy(step).start()
+
+        @pl.when(step > 0)
+        def _():
+            send_back(step - 1)
+
+        return carry
+
+    lax.fori_loop(0, down_steps, down_body, 0)
+    send_back(down_steps - 1)
+
+    for step in range(down_steps):
+        for distance in range(1, experts):
+            back_copy(step, distance).wait_recv()
+        mixed = jnp.dot(
+            share_ref[...],
+            back_in[step].reshape(packed, LANES).astype(jnp.float32),
+            precision=lax.Precision.HIGHEST,
+            preferred_element_type=jnp.float32,
+        )
+        for i in range(fold):
+            span = slice(step * down_step + i * LANES, step * down_step + (i + 1) * LANES)
+            out_ref[:, span] = (
+                hidden_ref[:, span] + mixed[i * rows : (i + 1) * rows]
+            ).astype(jnp.bfloat16)
+
+    for copy in attn_copies + slot_copies + pass_copies:
+        copy.wait_send()
+    for step in range(down_steps):
+        half_copy(step).wait_send()
+        for distance in range(1, experts):
+            back_copy(step, distance).wait_send()
+
+
+def fused_shards(resid, attn_part, norm_gain, w_router, routes, w_gate, w_up, w_down):
+    tensor_ranks = lax.axis_size("tensor")
+    rows, features = resid.shape
+    capacity = rows // 2
+    fold = PACKED_ROWS // capacity
+    width = features // fold
+    hidden_units = w_gate.shape[1]
+    step = fold * LANES
+    hidden_steps, down_steps = hidden_units // step, features // step
+    down_slots = min(down_steps, 4)
+    hidden_bytes, down_bytes = 4 * features * step, 2 * hidden_units * step
+    hidden_slots = min(hidden_steps, (WEIGHT_BYTES - down_slots * down_bytes) // hidden_bytes)
+    dma = pltpu.SemaphoreType.DMA
+    bf16, f32 = jnp.bfloat16, jnp.float32
+    half_rows = E * capacity
+    weights = 2 * features * hidden_units + hidden_units * features
+    return pl.pallas_call(
+        functools.partial(fused_kernel, (E, tensor_ranks, capacity, hidden_slots, down_slots)),
+        out_shape=jax.ShapeDtypeStruct(resid.shape, bf16),
+        in_specs=[pl.BlockSpec(memory_space=pl.ANY)] * 8,
+        out_specs=pl.BlockSpec(memory_space=pltpu.VMEM),
+        scratch_shapes=[
+            pltpu.VMEM(resid.shape, bf16),
+            pltpu.VMEM(attn_part.shape, bf16),
+            pltpu.VMEM((1, features), f32),
+            pltpu.VMEM(w_router.shape, bf16),
+            pltpu.VMEM(routes.shape, jnp.int32),
+            dma((5,)),
+            pltpu.VMEM((hidden_slots, 2, features, step), bf16),
+            dma((hidden_slots, 2)),
+            pltpu.VMEM((down_slots, hidden_units, step), bf16),
+            dma((down_slots,)),
+            pltpu.VMEM((tensor_ranks, 2 * rows, features // 2), bf16),
+            pltpu.VMEM((tensor_ranks - 1, 2 * rows, features // 2), bf16),
+            dma((tensor_ranks - 1,)),
+            dma((tensor_ranks - 1,)),
+            pltpu.VMEM(resid.shape, f32),
+            pltpu.VMEM((fold * rows, E * PACKED_ROWS), f32),
+            pltpu.VMEM((E, PACKED_ROWS, width), bf16),
+            pltpu.VMEM((2, E, PACKED_ROWS, width), bf16),
+            dma((E,)),
+            dma((E,)),
+            dma((E,)),
+            dma((E,)),
+            pltpu.VMEM((2 * half_rows, features), bf16),
+            pltpu.VMEM((2 * half_rows, hidden_units), bf16),
+            pltpu.VMEM((down_steps, 2, half_rows, step), f32),
+            pltpu.VMEM((down_steps, half_rows, step), bf16),
+            pltpu.VMEM((down_steps, half_rows, step), bf16),
+            dma((down_steps,)),
+            dma((down_steps,)),
+            pltpu.VMEM((down_steps, E, PACKED_ROWS, LANES), bf16),
+            pltpu.VMEM((down_steps, E, PACKED_ROWS, LANES), bf16),
+            dma((down_steps, E)),
+            dma((down_steps, E)),
+        ],
+        compiler_params=pltpu.CompilerParams(
+            collective_id=0, has_side_effects=True, vmem_limit_bytes=VMEM_BYTES
+        ),
+        cost_estimate=pl.CostEstimate(
+            flops=2 * 2 * half_rows * weights,
+            bytes_accessed=2 * weights,
+            transcendentals=2 * half_rows * hidden_units,
+        ),
+    )(resid, attn_part, norm_gain.reshape(1, features), w_router, routes, w_gate, w_up, w_down)
+
+
+def fits(mesh):
+    ranks = mesh.shape["expert"] * mesh.shape["tensor"]
+    return ranks == 2 * E and mesh.shape["tensor"] % 2 == 0
+
+
 def solution(mesh):
     return jax.shard_map(
-        shards,
+        fused_shards if fits(mesh) else shards,
         mesh=mesh,
         in_specs=(
             P(("groups", "expert", "tensor"), None),

time: 130 us -> 50.1 us (0.39)
  waiting for transfers between devices: 54.6 us -> 0 us
  Pallas kernels: 0 us -> 45.1 us
  matrix products: 33.9 us -> 0 us
  blocking collectives: 19.7 us -> 0 us
  between operations: 13.5 us -> 0.01 us
  starting transfers between devices: 4.58 us -> 0 us
  local copies, waits for them, and re-layouts: 2.53 us -> 4.72 us
    reduce_scatter x2 -> x0, waiting for transfers between devices: 46.5 us -> none  [the longest x1 24 us: shards(): lax.psum_scatter(partial_terms.astype(jnp.bfloat16), 'tensor', scatter_di...]
    pallas_call x0 -> x1, Pallas kernels: none -> 45.1 us  [fused_shards(): pl.pallas_call(functools.partial(fused_kernel, (E, tensor_ranks, capacity...]
    dot_general x6 -> x0, matrix products: 33.9 us -> none  [the longest x1 19.9 us: expert_partial(): jnp.dot(activated, w_down, preferred_element_type=jnp.float32)]
    all_to_all x1 -> x0, blocking collectives: 12.1 us -> none  [shards(): lax.all_to_all(own_sources.astype(jnp.bfloat16), 'expert', split_axis=0,...]
    all_gather x1 -> x0, blocking collectives: 7.66 us -> none  [shards(): lax.all_gather(arrived, 'tensor', axis=0, tiled=True)]
    all_to_all x1 -> x0, waiting for transfers between devices: 7.33 us -> none  [shards(): lax.all_to_all(outgoing, 'expert', split_axis=0, concat_axis=0, tiled=True)]
    all_to_all x1 -> x0, starting transfers between devices: 4.58 us -> none  [shards(): lax.all_to_all(outgoing, 'expert', split_axis=0, concat_axis=0, tiled=True)]
    unnamed x4 -> x3, local copies, waits for them, and re-layouts: 0.87 us -> 4.72 us
  transfers between devices with their start and end apart: 3 -> 0, of which waited for: 3 -> 0; matrix products, arithmetic and copies ran while one was open for 1% -> 0% of each run, Pallas kernels for 0% -> 0%
where the time goes in v1:
time: 50.1 us; the launch traced here: 49.9 us
  Pallas kernels  45.1 us (90%)
  local copies, waits for them, and re-layouts  4.72 us (9%)
    pallas_call x1, Pallas kernels, fused_shards(): pl.pallas_call(functools.partial(fused_kernel, (E, tensor_ranks, capacity...  45.1 us
    unnamed x3, local copies, waits for them, and re-layouts  4.72 us

profile of v1, /device:TPU:0, one launch (start us, length us, event | category | flops | bytes accessed | tf_op | source)
XLA Modules:
  0.0 49.9 jit_solution(17092563899375997156)
XLA Ops:
  0.0 1.3 %copy.10.routes_hbm = s32[8,2]{1,0:T(8,128)} copy(s32[8,2]{0,1:T(2,128)} %param.12) | data formatting | bytes 128 | tf_op args[4]
  1.3 2.0 %copy.9.router_hbm = bf16[3072,8]{1,0:T(8,128)(2,1)} copy(bf16[3072,8]{0,1:T(8,128)(2,1)} %param.11) | data formatting | bytes 98304 | tf_op args[3]
  3.3 45.1 %shard_map.82 = bf16[8,3072]{1,0:T(8,128)(2,1)} custom-call(bf16[8,3072]{1,0:T(8,128)(2,1)} %resid_hbm.1, bf16[32,3072]{1,0:T(8,128)(2,1)} %attn_hbm.1, f32[1,3072]{1,0:T(1,128)} %bitcast.1, bf16[3072,8]{1,0:T(8,128)(2,1)} %copy.9.router_hbm, s32[8,2]{1,0:T(8,128)} %copy.10.routes_hbm, bf16[3072,4096]{1,0:T(8,128)(2,1)} %gate_hbm.1, ...), custom_call_target="tpu_custom_call" | custom-call | flops 4831838208 | bytes 75497472 | tf_op jit(solution)/shard_map/pallas_call | solution.py:491
  48.4 1.4 %copy.12 = bf16[8,3072]{1,0:T(8,128)(2,1)} copy(bf16[8,3072]{1,0:T(8,128)(2,1)} %shard_map.82) | data formatting | bytes 98304

commit v2 on v1

--- a/solution.py
+++ b/solution.py
@@ -125,7 +125,7 @@
 LANES = 128
 PACKED_ROWS = 16
 WEIGHT_BYTES = 52 << 20
-VMEM_BYTES = 60 << 20
+VMEM_BYTES = 61 << 20
 
 
 def fused_kernel(
@@ -162,6 +162,8 @@
     pass_out_sem,
     pass_in_sem,
     tokens,
+    gate_sum,
+    up_sum,
     activated,
     partial_ref,
     half_out,
@@ -176,9 +178,13 @@
     experts, tensor_ranks, capacity, hidden_slots, down_slots = sizes
     rows, features = resid.shape
     fold = PACKED_ROWS // capacity
-    width = features // fold
-    hidden_step = hidden_weights.shape[3]
-    hidden_steps = gate_hbm.shape[1] // hidden_step
+    parts = slots_out.shape[0]
+    part_features = features // parts
+    width = part_features // fold
+    hidden_step = hidden_weights.shape[2]
+    hidden_steps = features // hidden_step
+    part_steps = hidden_steps // parts
+    hidden_units = gate_hbm.shape[1]
     down_step = down_weights.shape[2]
     down_steps = features // down_step
     pairs = tensor_ranks // 2
@@ -214,10 +220,10 @@
         copy.start()
 
     def hidden_copies(step, slot):
-        columns = pl.ds(pl.multiple_of(step * hidden_step, hidden_step), hidden_step)
+        inputs = pl.ds(pl.multiple_of(step * hidden_step, hidden_step), hidden_step)
         return [
             pltpu.make_async_copy(
-                source.at[:, columns], hidden_weights.at[slot, i], hidden_sem.at[slot, i]
+                source.at[inputs], hidden_weights.at[slot, i], hidden_sem.at[slot, i]
             )
             for i, source in enumerate((gate_hbm, up_hbm))
         ]
@@ -264,8 +270,14 @@
         copy.start()
     for copy in small[1:]:
         copy.wait()
-    route = routes[...]
-    first, second = route[:, 0:1], route[:, 1:2]
+    diagonal = lax.broadcasted_iota(jnp.int32, (rows, rows), 0) == lax.broadcasted_iota(
+        jnp.int32, (rows, rows), 1
+    )
+    first, second = [
+        jnp.sum(jnp.where(diagonal, routes[i : i + 1].astype(jnp.float32), 0.0), axis=1, keepdims=True)
+        .astype(jnp.int32)
+        for i in range(2)
+    ]
     columns = lax.broadcasted_iota(jnp.int32, (rows, LANES), 1)
     row_number = lax.broadcasted_iota(jnp.int32, (rows, LANES), 0)
     pick_first = (columns == first).astype(jnp.float32)
@@ -297,43 +309,51 @@
     mean_square = jnp.sum(hidden_wide * hidden_wide, axis=1, keepdims=True) / features
     normed_wide = hidden_wide * lax.rsqrt(mean_square + EPSILON) * gain[...]
     normed = normed_wide.astype(jnp.bfloat16)
-    folded = jnp.concatenate(
-        [normed_wide[:, i * width : (i + 1) * width] for i in range(fold)], axis=0
-    ).astype(jnp.bfloat16)
-    outgoing = jnp.dot(placement, folded, preferred_element_type=jnp.float32)
-    slots_out[...] = outgoing.astype(jnp.bfloat16).reshape(experts, PACKED_ROWS, width)
-
-    def slot_copy(step):
+
+    def slot_copy(part, step):
         return pltpu.make_async_remote_copy(
-            src_ref=slots_out.at[after(step)],
-            dst_ref=slots_in.at[core, me],
-            send_sem=slots_out_sem.at[step],
-            recv_sem=slots_in_sem.at[step],
+            src_ref=slots_out.at[part, after(step)],
+            dst_ref=slots_in.at[part, core, me],
+            send_sem=slots_out_sem.at[part, step],
+            recv_sem=slots_in_sem.at[part, step],
             device_id=holder(after(step)),
             device_id_type=MESH,
         )
 
-    def pass_copy(step):
-        source = slots_out.at[me] if step == 0 else slots_in.at[core, before(step)]
+    def pass_copy(part, step):
+        source = slots_out.at[part, me] if step == 0 else slots_in.at[part, core, before(step)]
         return pltpu.make_async_remote_copy(
             src_ref=source,
-            dst_ref=slots_in.at[core, before(step)],
-            send_sem=pass_out_sem.at[step],
-            recv_sem=pass_in_sem.at[step],
+            dst_ref=slots_in.at[part, core, before(step)],
+            send_sem=pass_out_sem.at[part, step],
+            recv_sem=pass_in_sem.at[part, step],
             device_id=sibling,
             device_id_type=MESH,
         )
 
-    slot_copies = [slot_copy(step) for step in range(1, experts)]
-    for copy in slot_copies:
-        copy.start()
-    pass_copies = [pass_copy(step) for step in range(experts)]
-    pass_copies[0].start()
+    for part in range(parts):
+        start = part * part_features
+        folded = jnp.concatenate(
+            [
+                normed_wide[:, start + i * width : start + (i + 1) * width]
+                for i in range(fold)
+            ],
+            axis=0,
+        ).astype(jnp.bfloat16)
+        outgoing = jnp.dot(placement, folded, preferred_element_type=jnp.float32)
+        slots_out[part] = outgoing.astype(jnp.bfloat16).reshape(experts, PACKED_ROWS, width)
+        for step in range(1, experts):
+            slot_copy(part, step).start()
+        pass_copy(part, 0).start()
+        slots_in[part, core, me] = slots_out[part, me]
     for step in range(down_slots):
         down_copy(step, step).start()
-    slots_in[core, me] = slots_out[me]
-
-    logits = jnp.dot(normed, router[...], preferred_element_type=jnp.float32)
+    gate_sum[...] = jnp.zeros_like(gate_sum)
+    up_sum[...] = jnp.zeros_like(up_sum)
+
+    logits = lax.dot_general(
+        normed, router[...], (((1,), (1,)), ((), ())), preferred_element_type=jnp.float32
+    )
     expert_columns = lax.broadcasted_iota(jnp.int32, (rows, experts), 1)
     logit_first = jnp.sum(jnp.where(expert_columns == first, logits, 0.0), axis=1, keepdims=True)
     logit_second = jnp.sum(jnp.where(expert_columns == second, logits, 0.0), axis=1, keepdims=True)
@@ -344,36 +364,44 @@
         + jnp.concatenate([share_second] * fold, axis=0) * cell_second
     )
 
-    for step in range(1, experts):
-        slot_copies[step - 1].wait_recv()
-        pass_copies[step].start()
-    for copy in pass_copies:
-        copy.wait_recv()
-
     sources = 2 * experts
     token_rows = sources * capacity
-    arrived = slots_in[...].reshape(sources * PACKED_ROWS, width)
     token_number = lax.broadcasted_iota(jnp.int32, (token_rows, sources * PACKED_ROWS), 0)
     packed_number = lax.broadcasted_iota(jnp.int32, (token_rows, sources * PACKED_ROWS), 1)
     wanted = token_number // capacity * PACKED_ROWS + token_number % capacity
-    for i in range(fold):
-        select = (packed_number == wanted + i * capacity).astype(jnp.float32).astype(jnp.bfloat16)
-        tokens[:, i * width : (i + 1) * width] = jnp.dot(
-            select, arrived, preferred_element_type=jnp.float32
-        ).astype(jnp.bfloat16)
+
+    def receive(part):
+        for step in range(1, experts):
+            slot_copy(part, step).wait_recv()
+            pass_copy(part, step).start()
+        for step in range(experts):
+            pass_copy(part, step).wait_recv()
+        arrived = slots_in[part].reshape(sources * PACKED_ROWS, width)
+        for i in range(fold):
+            select = (packed_number == wanted + i * capacity).astype(jnp.float32)
+            place, column = divmod(i * width, hidden_step)
+            tokens[part * part_steps + place, :, column : column + width] = jnp.dot(
+                select.astype(jnp.bfloat16), arrived, preferred_element_type=jnp.float32
+            ).astype(jnp.bfloat16)
+
+    tile = min(hidden_units, 8 * LANES)
 
     def hidden_body(step, carry):
         slot = step % hidden_slots
+
+        @pl.when(step % part_steps == 0)
+        def _():
+            receive(step // part_steps)
+
         for copy in hidden_copies(step, slot):
             copy.wait()
-        gate_value = jnp.dot(
-            tokens[...], hidden_weights[slot, 0], preferred_element_type=jnp.float32
-        )
-        up_value = jnp.dot(tokens[...], hidden_weights[slot, 1], preferred_element_type=jnp.float32)
-        value = gate_value / (1.0 + jnp.exp(-gate_value)) * up_value
-        activated[:, pl.ds(pl.multiple_of(step * hidden_step, hidden_step), hidden_step)] = (
-            value.astype(jnp.bfloat16)
-        )
+        for i, total in enumerate((gate_sum, up_sum)):
+            for start in range(0, hidden_units, tile):
+                total[:, start : start + tile] += jnp.dot(
+                    tokens[step],
+                    hidden_weights[slot, i, :, start : start + tile],
+                    preferred_element_type=jnp.float32,
+                )
 
         @pl.when(step + hidden_slots < hidden_steps)
         def _():
@@ -383,6 +411,11 @@
         return carry
 
     lax.fori_loop(0, hidden_steps, hidden_body, 0)
+    for start in range(0, hidden_units, tile):
+        span = slice(start, start + tile)
+        gate_value = gate_sum[:, span]
+        value = gate_value / (1.0 + jnp.exp(-gate_value)) * up_sum[:, span]
+        activated[:, span] = value.astype(jnp.bfloat16)
 
     half_rows = experts * capacity
 
@@ -464,8 +497,13 @@
                 hidden_ref[:, span] + mixed[i * rows : (i + 1) * rows]
             ).astype(jnp.bfloat16)
 
-    for copy in attn_copies + slot_copies + pass_copies:
+    for copy in attn_copies:
         copy.wait_send()
+    for part in range(parts):
+        for step in range(experts):
+            pass_copy(part, step).wait_send()
+            if step > 0:
+                slot_copy(part, step).wait_send()
     for step in range(down_steps):
         half_copy(step).wait_send()
         for distance in range(1, experts):
@@ -477,12 +515,14 @@
     rows, features = resid.shape
     capacity = rows // 2
     fold = PACKED_ROWS // capacity
-    width = features // fold
     hidden_units = w_gate.shape[1]
     step = fold * LANES
-    hidden_steps, down_steps = hidden_units // step, features // step
-    down_slots = min(down_steps, 4)
-    hidden_bytes, down_bytes = 4 * features * step, 2 * hidden_units * step
+    steps = features // step
+    parts = steps // 2 if steps % 2 == 0 else steps
+    width = features // parts // fold
+    hidden_steps, down_steps = steps, steps
+    down_slots = min(down_steps, 3)
+    hidden_bytes, down_bytes = 4 * hidden_units * step, 2 * hidden_units * step
     hidden_slots = min(hidden_steps, (WEIGHT_BYTES - down_slots * down_bytes) // hidden_bytes)
     dma = pltpu.SemaphoreType.DMA
     bf16, f32 = jnp.bfloat16, jnp.float32
@@ -497,10 +537,10 @@
             pltpu.VMEM(resid.shape, bf16),
             pltpu.VMEM(attn_part.shape, bf16),
             pltpu.VMEM((1, features), f32),
-            pltpu.VMEM(w_router.shape, bf16),
-            pltpu.VMEM(routes.shape, jnp.int32),
+            pltpu.VMEM(w_router.shape[::-1], bf16),
+            pltpu.VMEM(routes.shape[::-1], jnp.int32),
             dma((5,)),
-            pltpu.VMEM((hidden_slots, 2, features, step), bf16),
+            pltpu.VMEM((hidden_slots, 2, step, hidden_units), bf16),
             dma((hidden_slots, 2)),
             pltpu.VMEM((down_slots, hidden_units, step), bf16),
             dma((down_slots,)),
@@ -510,13 +550,15 @@
             dma((tensor_ranks - 1,)),
             pltpu.VMEM(resid.shape, f32),
             pltpu.VMEM((fold * rows, E * PACKED_ROWS), f32),
-            pltpu.VMEM((E, PACKED_ROWS, width), bf16),
-            pltpu.VMEM((2, E, PACKED_ROWS, width), bf16),
-            dma((E,)),
-            dma((E,)),
-            dma((E,)),
-            dma((E,)),
-            pltpu.VMEM((2 * half_rows, features), bf16),
+            pltpu.VMEM((parts, E, PACKED_ROWS, width), bf16),
+            pltpu.VMEM((parts, 2, E, PACKED_ROWS, width), bf16),
+            dma((parts, E)),
+            dma((parts, E)),
+            dma((parts, E)),
+            dma((parts, E)),
+            pltpu.VMEM((hidden_steps, 2 * half_rows, step), bf16),
+            pltpu.VMEM((2 * half_rows, hidden_units), f32),
+            pltpu.VMEM((2 * half_rows, hidden_units), f32),
             pltpu.VMEM((2 * half_rows, hidden_units), bf16),
             pltpu.VMEM((down_steps, 2, half_rows, step), f32),
             pltpu.VMEM((down_steps, half_rows, step), bf16),
@@ -536,7 +578,7 @@
             bytes_accessed=2 * weights,
             transcendentals=2 * half_rows * hidden_units,
         ),
-    )(resid, attn_part, norm_gain.reshape(1, features), w_router, routes, w_gate, w_up, w_down)
+    )(resid, attn_part, norm_gain.reshape(1, features), w_router.T, routes.T, w_gate, w_up, w_down)
 
 
 def fits(mesh):

time: 50.1 us -> 49.5 us (0.988)
  local copies, waits for them, and re-layouts: 4.72 us -> 1.42 us
  Pallas kernels: 45.1 us -> 47.9 us
    unnamed x3 -> x1, local copies, waits for them, and re-layouts: 4.72 us -> 1.42 us
    pallas_call x1, Pallas kernels: 45.1 us -> 47.9 us  [fused_shards(): pl.pallas_call(functools.partial(fused_kernel, (E, tensor_ranks, capacity...]
where the time goes in v2:
time: 49.5 us; the launch traced here: 49.3 us
  Pallas kernels  47.9 us (97%)
  local copies, waits for them, and re-layouts  1.42 us (3%)
    pallas_call x1, Pallas kernels, fused_shards(): pl.pallas_call(functools.partial(fused_kernel, (E, tensor_ranks, capacity...  47.9 us
    unnamed x1, local copies, waits for them, and re-layouts  1.42 us

profile of v2, /device:TPU:0, one launch (start us, length us, event | category | flops | bytes accessed | tf_op | source)
XLA Modules:
  0.0 49.3 jit_solution(16872419371085110321)
XLA Ops:
  0.0 47.9 %shard_map.82 = bf16[8,3072]{1,0:T(8,128)(2,1)} custom-call(bf16[8,3072]{1,0:T(8,128)(2,1)} %resid_hbm.1, bf16[32,3072]{1,0:T(8,128)(2,1)} %attn_hbm.1, f32[1,3072]{1,0:T(1,128)} %bitcast.4, bf16[8,3072]{1,0:T(8,128)(2,1)} %bitcast.3, s32[2,8]{1,0:T(2,128)} %bitcast.5, bf16[3072,4096]{1,0:T(8,128)(2,1)} %gate_hbm.1, bf16[3072,4096]{1,0:T(8,128)(2,1)} %up_hbm.1, ...), custom_call_target="tpu_custom_call" | custom-call | flops 4831838208 | bytes 75497472 | tf_op jit(solution)/shard_map/pallas_call | solution.py:531
  47.9 1.4 %copy.10 = bf16[8,3072]{1,0:T(8,128)(2,1)} copy(bf16[8,3072]{1,0:T(8,128)(2,1)} %shard_map.82) | data formatting | bytes 98304

commit v3 on v1

--- a/solution.py
+++ b/solution.py
@@ -180,7 +180,10 @@
     hidden_step = hidden_weights.shape[3]
     hidden_steps = gate_hbm.shape[1] // hidden_step
     down_step = down_weights.shape[2]
-    down_steps = features // down_step
+    chunks, _, _, chunk = partial_ref.shape
+    chunk_steps = chunk // down_step
+    down_steps = chunks * chunk_steps
+    span = chunk // fold
     pairs = tensor_ranks // 2
     group = lax.axis_index("groups")
     my_z = lax.axis_index("expert")
@@ -213,6 +216,12 @@
     for copy in small:
         copy.start()
 
+    barrier = pltpu.get_barrier_semaphore()
+    tensor_peers = [(group, my_z, (my_t + i) % tensor_ranks) for i in range(1, tensor_ranks, 2)]
+    peers = [holder(after(i)) for i in range(1, experts)]
+    for peer in tensor_peers + peers:
+        pl.semaphore_signal(barrier, inc=1, device_id=peer, device_id_type=MESH)
+
     def hidden_copies(step, slot):
         columns = pl.ds(pl.multiple_of(step * hidden_step, hidden_step), hidden_step)
         return [
@@ -231,12 +240,6 @@
     for step in range(hidden_slots):
         for copy in hidden_copies(step, step):
             copy.start()
-
-    barrier = pltpu.get_barrier_semaphore()
-    tensor_peers = [(group, my_z, (my_t + i) % tensor_ranks) for i in range(1, tensor_ranks)]
-    peers = [holder(after(i)) for i in range(1, experts)]
-    for peer in tensor_peers + peers:
-        pl.semaphore_signal(barrier, inc=1, device_id=peer, device_id_type=MESH)
 
     small[0].wait()
     terms = attn[...].astype(jnp.float32)
@@ -264,8 +267,14 @@
         copy.start()
     for copy in small[1:]:
         copy.wait()
-    route = routes[...]
-    first, second = route[:, 0:1], route[:, 1:2]
+    diagonal = lax.broadcasted_iota(jnp.int32, (rows, rows), 0) == lax.broadcasted_iota(
+        jnp.int32, (rows, rows), 1
+    )
+    first, second = [
+        jnp.sum(jnp.where(diagonal, routes[i : i + 1].astype(jnp.float32), 0.0), axis=1, keepdims=True)
+        .astype(jnp.int32)
+        for i in range(2)
+    ]
     columns = lax.broadcasted_iota(jnp.int32, (rows, LANES), 1)
     row_number = lax.broadcasted_iota(jnp.int32, (rows, LANES), 0)
     pick_first = (columns == first).astype(jnp.float32)
@@ -307,33 +316,38 @@
         return pltpu.make_async_remote_copy(
             src_ref=slots_out.at[after(step)],
             dst_ref=slots_in.at[core, me],
-            send_sem=slots_out_sem.at[step],
-            recv_sem=slots_in_sem.at[step],
+            send_sem=slots_out_sem,
+            recv_sem=slots_in_sem,
             device_id=holder(after(step)),
             device_id_type=MESH,
         )
 
-    def pass_copy(step):
-        source = slots_out.at[me] if step == 0 else slots_in.at[core, before(step)]
-        return pltpu.make_async_remote_copy(
-            src_ref=source,
-            dst_ref=slots_in.at[core, before(step)],
-            send_sem=pass_out_sem.at[step],
-            recv_sem=pass_in_sem.at[step],
-            device_id=sibling,
-            device_id_type=MESH,
-        )
-
-    slot_copies = [slot_copy(step) for step in range(1, experts)]
-    for copy in slot_copies:
-        copy.start()
-    pass_copies = [pass_copy(step) for step in range(experts)]
-    pass_copies[0].start()
+    others = pl.ds(0, experts - 1)
+    all_slots = pltpu.make_async_remote_copy(
+        src_ref=slots_out.at[others],
+        dst_ref=slots_in.at[core, others],
+        send_sem=slots_out_sem,
+        recv_sem=slots_in_sem,
+        device_id=sibling,
+        device_id_type=MESH,
+    )
+    pass_copy = pltpu.make_async_remote_copy(
+        src_ref=slots_in.at[core],
+        dst_ref=slots_in.at[core],
+        send_sem=pass_out_sem,
+        recv_sem=pass_in_sem,
+        device_id=sibling,
+        device_id_type=MESH,
+    )
+    for step in range(1, experts):
+        slot_copy(step).start()
     for step in range(down_slots):
         down_copy(step, step).start()
     slots_in[core, me] = slots_out[me]
 
-    logits = jnp.dot(normed, router[...], preferred_element_type=jnp.float32)
+    logits = lax.dot_general(
+        normed, router[...], (((1,), (1,)), ((), ())), preferred_element_type=jnp.float32
+    )
     expert_columns = lax.broadcasted_iota(jnp.int32, (rows, experts), 1)
     logit_first = jnp.sum(jnp.where(expert_columns == first, logits, 0.0), axis=1, keepdims=True)
     logit_second = jnp.sum(jnp.where(expert_columns == second, logits, 0.0), axis=1, keepdims=True)
@@ -344,11 +358,9 @@
         + jnp.concatenate([share_second] * fold, axis=0) * cell_second
     )
 
-    for step in range(1, experts):
-        slot_copies[step - 1].wait_recv()
-        pass_copies[step].start()
-    for copy in pass_copies:
-        copy.wait_recv()
+    all_slots.wait_recv()
+    pass_copy.start()
+    pass_copy.wait_recv()
 
     sources = 2 * experts
     token_rows = sources * capacity
@@ -400,9 +412,19 @@
         return pltpu.make_async_remote_copy(
             src_ref=back_out.at[step, after(distance)],
             dst_ref=back_in.at[step, me],
-            send_sem=back_out_sem.at[step, distance],
-            recv_sem=back_in_sem.at[step, distance],
+            send_sem=back_out_sem.at[step],
+            recv_sem=back_in_sem.at[step],
             device_id=holder(after(distance)),
+            device_id_type=MESH,
+        )
+
+    def all_back(step):
+        return pltpu.make_async_remote_copy(
+            src_ref=back_out.at[step, others],
+            dst_ref=back_in.at[step, others],
+            send_sem=back_out_sem.at[step],
+            recv_sem=back_in_sem.at[step],
+            device_id=sibling,
             device_id_type=MESH,
         )
 
@@ -419,57 +441,62 @@
         half_copy(step).wait_recv()
         total = partial_ref[step, core] + half_in[step].astype(jnp.float32)
         stacked = jnp.concatenate(
-            [total[:, i * LANES : (i + 1) * LANES] for i in range(fold)], axis=0
+            [total[:, i * span : (i + 1) * span] for i in range(fold)], axis=0
         ).astype(jnp.bfloat16)
         ordered = jnp.dot(reorder, stacked, preferred_element_type=jnp.float32)
-        back_out[step] = ordered.astype(jnp.bfloat16).reshape(experts, PACKED_ROWS, LANES)
+        back_out[step] = ordered.astype(jnp.bfloat16).reshape(experts, PACKED_ROWS, span)
         for distance in range(1, experts):
             back_copy(step, distance).start()
         back_in[step, me] = back_out[step, me]
 
     def down_body(step, carry):
-        slot = step % down_slots
-        down_copy(step, slot).wait()
-        produced = jnp.dot(activated[...], down_weights[slot], preferred_element_type=jnp.float32)
-        partial_ref[step] = produced.reshape(2, half_rows, down_step)
-
-        @pl.when(step + down_slots < down_steps)
-        def _():
-            down_copy(step + down_slots, slot).start()
+        for i in range(chunk_steps):
+            piece = step * chunk_steps + i
+            slot = piece % down_slots
+            down_copy(piece, slot).wait()
+            produced = jnp.dot(
+                activated[...], down_weights[slot], preferred_element_type=jnp.float32
+            )
+            partial_ref[step, :, :, i * down_step : (i + 1) * down_step] = produced.reshape(
+                2, half_rows, down_step
+            )
+
+            @pl.when(piece + down_slots < down_steps)
+            def _():
+                down_copy(piece + down_slots, slot).start()
+
+            if i == 0:
+
+                @pl.when(step > 0)
+                def _():
+                    send_back(step - 1)
 
         half_out[step] = partial_ref[step, 1 - core].astype(jnp.bfloat16)
         half_copy(step).start()
-
-        @pl.when(step > 0)
-        def _():
-            send_back(step - 1)
-
         return carry
 
-    lax.fori_loop(0, down_steps, down_body, 0)
-    send_back(down_steps - 1)
-
-    for step in range(down_steps):
-        for distance in range(1, experts):
-            back_copy(step, distance).wait_recv()
+    lax.fori_loop(0, chunks, down_body, 0)
+    send_back(chunks - 1)
+
+    for step in range(chunks):
+        all_back(step).wait_recv()
         mixed = jnp.dot(
             share_ref[...],
-            back_in[step].reshape(packed, LANES).astype(jnp.float32),
+            back_in[step].reshape(packed, span).astype(jnp.float32),
             precision=lax.Precision.HIGHEST,
             preferred_element_type=jnp.float32,
         )
         for i in range(fold):
-            span = slice(step * down_step + i * LANES, step * down_step + (i + 1) * LANES)
-            out_ref[:, span] = (
-                hidden_ref[:, span] + mixed[i * rows : (i + 1) * rows]
+            where = slice(step * chunk + i * span, step * chunk + (i + 1) * span)
+            out_ref[:, where] = (
+                hidden_ref[:, where] + mixed[i * rows : (i + 1) * rows]
             ).astype(jnp.bfloat16)
 
-    for copy in attn_copies + slot_copies + pass_copies:
+    for copy in attn_copies + [all_slots, pass_copy]:
         copy.wait_send()
-    for step in range(down_steps):
+    for step in range(chunks):
         half_copy(step).wait_send()
-        for distance in range(1, experts):
-            back_copy(step, distance).wait_send()
+        all_back(step).wait_send()
 
 
 def fused_shards(resid, attn_part, norm_gain, w_router, routes, w_gate, w_up, w_down):
@@ -482,6 +509,8 @@
     step = fold * LANES
     hidden_steps, down_steps = hidden_units // step, features // step
     down_slots = min(down_steps, 4)
+    chunk = 2 * step if down_steps % 2 == 0 else step
+    chunks = features // chunk
     hidden_bytes, down_bytes = 4 * features * step, 2 * hidden_units * step
     hidden_slots = min(hidden_steps, (WEIGHT_BYTES - down_slots * down_bytes) // hidden_bytes)
     dma = pltpu.SemaphoreType.DMA
@@ -497,8 +526,8 @@
             pltpu.VMEM(resid.shape, bf16),
             pltpu.VMEM(attn_part.shape, bf16),
             pltpu.VMEM((1, features), f32),
-            pltpu.VMEM(w_router.shape, bf16),
-            pltpu.VMEM(routes.shape, jnp.int32),
+            pltpu.VMEM(w_router.shape[::-1], bf16),
+            pltpu.VMEM(routes.shape[::-1], jnp.int32),
             dma((5,)),
             pltpu.VMEM((hidden_slots, 2, features, step), bf16),
             dma((hidden_slots, 2)),
@@ -512,21 +541,21 @@
             pltpu.VMEM((fold * rows, E * PACKED_ROWS), f32),
             pltpu.VMEM((E, PACKED_ROWS, width), bf16),
             pltpu.VMEM((2, E, PACKED_ROWS, width), bf16),
-            dma((E,)),
-            dma((E,)),
-            dma((E,)),
-            dma((E,)),
+            dma(()),
+            dma(()),
+            dma(()),
+            dma(()),
             pltpu.VMEM((2 * half_rows, features), bf16),
             pltpu.VMEM((2 * half_rows, hidden_units), bf16),
-            pltpu.VMEM((down_steps, 2, half_rows, step), f32),
-            pltpu.VMEM((down_steps, half_rows, step), bf16),
-            pltpu.VMEM((down_steps, half_rows, step), bf16),
-            dma((down_steps,)),
-            dma((down_steps,)),
-            pltpu.VMEM((down_steps, E, PACKED_ROWS, LANES), bf16),
-            pltpu.VMEM((down_steps, E, PACKED_ROWS, LANES), bf16),
-            dma((down_steps, E)),
-            dma((down_steps, E)),
+            pltpu.VMEM((chunks, 2, half_rows, chunk), f32),
+            pltpu.VMEM((chunks, half_rows, chunk), bf16),
+            pltpu.VMEM((chunks, half_rows, chunk), bf16),
+            dma((chunks,)),
+            dma((chunks,)),
+            pltpu.VMEM((chunks, E, PACKED_ROWS, chunk // fold), bf16),
+            pltpu.VMEM((chunks, E, PACKED_ROWS, chunk // fold), bf16),
+            dma((chunks,)),
+            dma((chunks,)),
         ],
         compiler_params=pltpu.CompilerParams(
             collective_id=0, has_side_effects=True, vmem_limit_bytes=VMEM_BYTES
@@ -536,7 +565,7 @@
             bytes_accessed=2 * weights,
             transcendentals=2 * half_rows * hidden_units,
         ),
-    )(resid, attn_part, norm_gain.reshape(1, features), w_router, routes, w_gate, w_up, w_down)
+    )(resid, attn_part, norm_gain.reshape(1, features), w_router.T, routes.T, w_gate, w_up, w_down)
 
 
 def fits(mesh):

time: 50.1 us -> 40.9 us (0.82)
  Pallas kernels: 45.1 us -> 39.3 us
  local copies, waits for them, and re-layouts: 4.72 us -> 1.42 us
    pallas_call x1, Pallas kernels: 45.1 us -> 39.3 us  [fused_shards(): pl.pallas_call(functools.partial(fused_kernel, (E, tensor_ranks, capacity...]
    unnamed x3 -> x1, local copies, waits for them, and re-layouts: 4.72 us -> 1.42 us
where the time goes in v3:
time: 40.9 us; the launch traced here: 40.7 us
  Pallas kernels  39.3 us (96%)
  local copies, waits for them, and re-layouts  1.42 us (3%)
    pallas_call x1, Pallas kernels, fused_shards(): pl.pallas_call(functools.partial(fused_kernel, (E, tensor_ranks, capacity...  39.3 us
    unnamed x1, local copies, waits for them, and re-layouts  1.42 us

profile of v3, /device:TPU:0, one launch (start us, length us, event | category | flops | bytes accessed | tf_op | source)
XLA Modules:
  0.0 40.7 jit_solution(16430395257467731012)
XLA Ops:
  0.0 39.3 %shard_map.82 = bf16[8,3072]{1,0:T(8,128)(2,1)} custom-call(bf16[8,3072]{1,0:T(8,128)(2,1)} %resid_hbm.1, bf16[32,3072]{1,0:T(8,128)(2,1)} %attn_hbm.1, f32[1,3072]{1,0:T(1,128)} %bitcast.4, bf16[8,3072]{1,0:T(8,128)(2,1)} %bitcast.3, s32[2,8]{1,0:T(2,128)} %bitcast.5, bf16[3072,4096]{1,0:T(8,128)(2,1)} %gate_hbm.1, bf16[3072,4096]{1,0:T(8,128)(2,1)} %up_hbm.1, ...), custom_call_target="tpu_custom_call" | custom-call | flops 4831838208 | bytes 75497472 | tf_op jit(solution)/shard_map/pallas_call | solution.py:520
  39.3 1.4 %copy.10 = bf16[8,3072]{1,0:T(8,128)(2,1)} copy(bf16[8,3072]{1,0:T(8,128)(2,1)} %shard_map.82) | data formatting | bytes 98304

commit v4 on v3

--- a/solution.py
+++ b/solution.py
@@ -161,6 +161,8 @@
     slots_in_sem,
     pass_out_sem,
     pass_in_sem,
+    select,
+    reorder,
     tokens,
     activated,
     partial_ref,
@@ -237,10 +239,11 @@
             down_hbm.at[:, columns], down_weights.at[slot], down_sem.at[slot]
         )
 
-    for step in range(hidden_slots):
+    def start_hidden(step):
         for copy in hidden_copies(step, step):
             copy.start()
 
+    start_hidden(0)
     small[0].wait()
     terms = attn[...].astype(jnp.float32)
     half = features // 2
@@ -265,6 +268,8 @@
     attn_copies = [attn_copy(step) for step in range(1, tensor_ranks)]
     for copy in attn_copies:
         copy.start()
+    for step in range(1, min(2, hidden_slots)):
+        start_hidden(step)
     for copy in small[1:]:
         copy.wait()
     diagonal = lax.broadcasted_iota(jnp.int32, (rows, rows), 0) == lax.broadcasted_iota(
@@ -339,8 +344,10 @@
         device_id=sibling,
         device_id_type=MESH,
     )
-    for step in range(1, experts):
+    for step in sorted(range(1, experts), key=lambda step: abs(2 * step - experts - 1)):
         slot_copy(step).start()
+    for step in range(2, hidden_slots):
+        start_hidden(step)
     for step in range(down_slots):
         down_copy(step, step).start()
     slots_in[core, me] = slots_out[me]
@@ -358,34 +365,54 @@
         + jnp.concatenate([share_second] * fold, axis=0) * cell_second
     )
 
-    all_slots.wait_recv()
-    pass_copy.start()
-    pass_copy.wait_recv()
-
     sources = 2 * experts
     token_rows = sources * capacity
-    arrived = slots_in[...].reshape(sources * PACKED_ROWS, width)
     token_number = lax.broadcasted_iota(jnp.int32, (token_rows, sources * PACKED_ROWS), 0)
     packed_number = lax.broadcasted_iota(jnp.int32, (token_rows, sources * PACKED_ROWS), 1)
     wanted = token_number // capacity * PACKED_ROWS + token_number % capacity
     for i in range(fold):
-        select = (packed_number == wanted + i * capacity).astype(jnp.float32).astype(jnp.bfloat16)
+        select[i] = (
+            (packed_number == wanted + i * capacity).astype(jnp.float32).astype(jnp.bfloat16)
+        )
+    half_rows = experts * capacity
+    to_row = lax.broadcasted_iota(jnp.int32, (packed, packed), 0)
+    from_row = lax.broadcasted_iota(jnp.int32, (packed, packed), 1)
+    origin = (
+        to_row % PACKED_ROWS // capacity * half_rows
+        + to_row // PACKED_ROWS * capacity
+        + to_row % capacity
+    )
+    reorder[...] = (from_row == origin).astype(jnp.float32).astype(jnp.bfloat16)
+
+    all_slots.wait_recv()
+    pass_copy.start()
+    pass_copy.wait_recv()
+    arrived = slots_in[...].reshape(sources * PACKED_ROWS, width)
+    for i in range(fold):
         tokens[:, i * width : (i + 1) * width] = jnp.dot(
-            select, arrived, preferred_element_type=jnp.float32
+            select[i], arrived, preferred_element_type=jnp.float32
         ).astype(jnp.bfloat16)
+
+    tile = fold * LANES
 
     def hidden_body(step, carry):
         slot = step % hidden_slots
         for copy in hidden_copies(step, slot):
             copy.wait()
-        gate_value = jnp.dot(
-            tokens[...], hidden_weights[slot, 0], preferred_element_type=jnp.float32
-        )
-        up_value = jnp.dot(tokens[...], hidden_weights[slot, 1], preferred_element_type=jnp.float32)
-        value = gate_value / (1.0 + jnp.exp(-gate_value)) * up_value
-        activated[:, pl.ds(pl.multiple_of(step * hidden_step, hidden_step), hidden_step)] = (
-            value.astype(jnp.bfloat16)
-        )
+        for start in range(0, hidden_step, tile):
+            gate_value = jnp.dot(
+                tokens[...],
+                hidden_weights[slot, 0, :, start : start + tile],
+                preferred_element_type=jnp.float32,
+            )
+            up_value = jnp.dot(
+                tokens[...],
+                hidden_weights[slot, 1, :, start : start + tile],
+                preferred_element_type=jnp.float32,
+            )
+            value = gate_value / (1.0 + jnp.exp(-gate_value)) * up_value
+            where = pl.ds(pl.multiple_of(step * hidden_step + start, tile), tile)
+            activated[:, where] = value.astype(jnp.bfloat16)
 
         @pl.when(step + hidden_slots < hidden_steps)
         def _():
@@ -395,8 +422,6 @@
         return carry
 
     lax.fori_loop(0, hidden_steps, hidden_body, 0)
-
-    half_rows = experts * capacity
 
     def half_copy(step):
         return pltpu.make_async_remote_copy(
@@ -428,22 +453,13 @@
             device_id_type=MESH,
         )
 
-    to_row = lax.broadcasted_iota(jnp.int32, (packed, packed), 0)
-    from_row = lax.broadcasted_iota(jnp.int32, (packed, packed), 1)
-    origin = (
-        to_row % PACKED_ROWS // capacity * half_rows
-        + to_row // PACKED_ROWS * capacity
-        + to_row % capacity
-    )
-    reorder = (from_row == origin).astype(jnp.float32).astype(jnp.bfloat16)
-
     def send_back(step):
         half_copy(step).wait_recv()
         total = partial_ref[step, core] + half_in[step].astype(jnp.float32)
         stacked = jnp.concatenate(
             [total[:, i * span : (i + 1) * span] for i in range(fold)], axis=0
         ).astype(jnp.bfloat16)
-        ordered = jnp.dot(reorder, stacked, preferred_element_type=jnp.float32)
+        ordered = jnp.dot(reorder[...], stacked, preferred_element_type=jnp.float32)
         back_out[step] = ordered.astype(jnp.bfloat16).reshape(experts, PACKED_ROWS, span)
         for distance in range(1, experts):
             back_copy(step, distance).start()
@@ -476,9 +492,8 @@
         return carry
 
     lax.fori_loop(0, chunks, down_body, 0)
-    send_back(chunks - 1)
-
-    for step in range(chunks):
+
+    def combine(step):
         all_back(step).wait_recv()
         mixed = jnp.dot(
             share_ref[...],
@@ -491,6 +506,12 @@
             out_ref[:, where] = (
                 hidden_ref[:, where] + mixed[i * rows : (i + 1) * rows]
             ).astype(jnp.bfloat16)
+
+    for step in range(chunks - 2):
+        combine(step)
+    send_back(chunks - 1)
+    for step in range(max(0, chunks - 2), chunks):
+        combine(step)
 
     for copy in attn_copies + [all_slots, pass_copy]:
         copy.wait_send()
@@ -507,11 +528,12 @@
     width = features // fold
     hidden_units = w_gate.shape[1]
     step = fold * LANES
-    hidden_steps, down_steps = hidden_units // step, features // step
+    hidden_step = 2 * step if hidden_units % (2 * step) == 0 else step
+    hidden_steps, down_steps = hidden_units // hidden_step, features // step
     down_slots = min(down_steps, 4)
     chunk = 2 * step if down_steps % 2 == 0 else step
     chunks = features // chunk
-    hidden_bytes, down_bytes = 4 * features * step, 2 * hidden_units * step
+    hidden_bytes, down_bytes = 4 * features * hidden_step, 2 * hidden_units * step
     hidden_slots = min(hidden_steps, (WEIGHT_BYTES - down_slots * down_bytes) // hidden_bytes)
     dma = pltpu.SemaphoreType.DMA
     bf16, f32 = jnp.bfloat16, jnp.float32
@@ -529,7 +551,7 @@
             pltpu.VMEM(w_router.shape[::-1], bf16),
             pltpu.VMEM(routes.shape[::-1], jnp.int32),
             dma((5,)),
-            pltpu.VMEM((hidden_slots, 2, features, step), bf16),
+            pltpu.VMEM((hidden_slots, 2, features, hidden_step), bf16),
             dma((hidden_slots, 2)),
             pltpu.VMEM((down_slots, hidden_units, step), bf16),
             dma((down_slots,)),
@@ -545,6 +567,8 @@
             dma(()),
             dma(()),
             dma(()),
+            pltpu.VMEM((fold, 2 * half_rows, 2 * E * PACKED_ROWS), bf16),
+            pltpu.VMEM((E * PACKED_ROWS, E * PACKED_ROWS), bf16),
             pltpu.VMEM((2 * half_rows, features), bf16),
             pltpu.VMEM((2 * half_rows, hidden_units), bf16),
             pltpu.VMEM((chunks, 2, half_rows, chunk), f32),

time: 40.9 us -> 40.8 us (level)
  no operation moved by 1% of the time
where the time goes in v4:
time: 40.8 us; the launch traced here: 40.6 us
  Pallas kernels  39.2 us (96%)
  local copies, waits for them, and re-layouts  1.42 us (3%)
    pallas_call x1, Pallas kernels, fused_shards(): pl.pallas_call(functools.partial(fused_kernel, (E, tensor_ranks, capacity...  39.2 us
    unnamed x1, local copies, waits for them, and re-layouts  1.42 us

profile of v4, /device:TPU:0, one launch (start us, length us, event | category | flops | bytes accessed | tf_op | source)
XLA Modules:
  0.0 40.6 jit_solution(13868375708849883946)
XLA Ops:
  0.0 39.2 %shard_map.82 = bf16[8,3072]{1,0:T(8,128)(2,1)} custom-call(bf16[8,3072]{1,0:T(8,128)(2,1)} %resid_hbm.1, bf16[32,3072]{1,0:T(8,128)(2,1)} %attn_hbm.1, f32[1,3072]{1,0:T(1,128)} %bitcast.4, bf16[8,3072]{1,0:T(8,128)(2,1)} %bitcast.3, s32[2,8]{1,0:T(2,128)} %bitcast.5, bf16[3072,4096]{1,0:T(8,128)(2,1)} %gate_hbm.1, bf16[3072,4096]{1,0:T(8,128)(2,1)} %up_hbm.1, ...), custom_call_target="tpu_custom_call" | custom-call | flops 4831838208 | bytes 75497472 | tf_op jit(solution)/shard_map/pallas_call | solution.py:542
  39.2 1.4 %copy.10 = bf16[8,3072]{1,0:T(8,128)(2,1)} copy(bf16[8,3072]{1,0:T(8,128)(2,1)} %shard_map.82) | data formatting | bytes 98304

commit v5 on v4

--- a/solution.py
+++ b/solution.py
@@ -126,6 +126,10 @@
 PACKED_ROWS = 16
 WEIGHT_BYTES = 52 << 20
 VMEM_BYTES = 60 << 20
+
+
+def log(power):
+    return power.bit_length() - 1
 
 
 def fused_kernel(
@@ -190,18 +194,15 @@
     group = lax.axis_index("groups")
     my_z = lax.axis_index("expert")
     my_t = lax.axis_index("tensor")
-    core = my_t % 2
-    me = my_z * pairs + my_t // 2
+    core = lax.rem(my_t, 2)
+    me = my_z * pairs + lax.div(my_t, 2)
     sibling = (group, my_z, my_t + 1 - 2 * core)
 
-    def holder(number):
-        return (group, number // pairs, (number % pairs) * 2 + core)
-
-    def after(step):
-        return (me + step) % experts
-
-    def before(step):
-        return (me + experts - step) % experts
+    after = [lax.rem(me + step, experts) for step in range(experts)]
+    holder = [
+        (group, lax.div(number, pairs), lax.rem(number, pairs) * 2 + core) for number in after
+    ]
+    tensor_after = [lax.rem(my_t + step, tensor_ranks) for step in range(tensor_ranks)]
 
     small = [
         pltpu.make_async_copy(source, target, in_sem.at[i])
@@ -219,8 +220,8 @@
         copy.start()
 
     barrier = pltpu.get_barrier_semaphore()
-    tensor_peers = [(group, my_z, (my_t + i) % tensor_ranks) for i in range(1, tensor_ranks, 2)]
-    peers = [holder(after(i)) for i in range(1, experts)]
+    tensor_peers = [(group, my_z, tensor_after[i]) for i in range(1, tensor_ranks, 2)]
+    peers = holder[1:]
     for peer in tensor_peers + peers:
         pl.semaphore_signal(barrier, inc=1, device_id=peer, device_id_type=MESH)
 
@@ -255,7 +256,7 @@
     pl.semaphore_wait(barrier, len(tensor_peers) + len(peers))
 
     def attn_copy(step):
-        target = (my_t + step) % tensor_ranks
+        target = tensor_after[step]
         return pltpu.make_async_remote_copy(
             src_ref=attn_out.at[target],
             dst_ref=attn_in.at[step - 1],
@@ -293,7 +294,8 @@
     place_first = jnp.concatenate([first * PACKED_ROWS + slot_first] * fold, axis=0)
     place_second = jnp.concatenate([second * PACKED_ROWS + slot_second] * fold, axis=0)
     packed = experts * PACKED_ROWS
-    part = lax.broadcasted_iota(jnp.int32, (fold * rows, packed), 0) // rows * capacity
+    part = lax.broadcasted_iota(jnp.int32, (fold * rows, packed), 0)
+    part = (part >> log(rows)) * capacity
     cells = lax.broadcasted_iota(jnp.int32, (fold * rows, packed), 1) - part
     cell_first = (cells == place_first).astype(jnp.float32)
     cell_second = (cells == place_second).astype(jnp.float32)
@@ -319,11 +321,11 @@
 
     def slot_copy(step):
         return pltpu.make_async_remote_copy(
-            src_ref=slots_out.at[after(step)],
+            src_ref=slots_out.at[after[step]],
             dst_ref=slots_in.at[core, me],
             send_sem=slots_out_sem,
             recv_sem=slots_in_sem,
-            device_id=holder(after(step)),
+            device_id=holder[step],
             device_id_type=MESH,
         )
 
@@ -360,16 +362,20 @@
     logit_second = jnp.sum(jnp.where(expert_columns == second, logits, 0.0), axis=1, keepdims=True)
     share_first = 1.0 / (1.0 + jnp.exp(logit_second - logit_first))
     share_second = 1.0 - share_first
-    share_ref[...] = (
+    share = (
         jnp.concatenate([share_first] * fold, axis=0) * cell_first
         + jnp.concatenate([share_second] * fold, axis=0) * cell_second
     )
+    for i in range(3):
+        term = share.astype(jnp.bfloat16)
+        share_ref[i * fold * rows : (i + 1) * fold * rows] = term
+        share = share - term.astype(jnp.float32)
 
     sources = 2 * experts
     token_rows = sources * capacity
     token_number = lax.broadcasted_iota(jnp.int32, (token_rows, sources * PACKED_ROWS), 0)
     packed_number = lax.broadcasted_iota(jnp.int32, (token_rows, sources * PACKED_ROWS), 1)
-    wanted = token_number // capacity * PACKED_ROWS + token_number % capacity
+    wanted = (token_number >> log(capacity)) * PACKED_ROWS + (token_number & (capacity - 1))
     for i in range(fold):
         select[i] = (
             (packed_number == wanted + i * capacity).astype(jnp.float32).astype(jnp.bfloat16)
@@ -378,9 +384,9 @@
     to_row = lax.broadcasted_iota(jnp.int32, (packed, packed), 0)
     from_row = lax.broadcasted_iota(jnp.int32, (packed, packed), 1)
     origin = (
-        to_row % PACKED_ROWS // capacity * half_rows
-        + to_row // PACKED_ROWS * capacity
-        + to_row % capacity
+        ((to_row & (PACKED_ROWS - 1)) >> log(capacity)) * half_rows
+        + (to_row >> log(PACKED_ROWS)) * capacity
+        + (to_row & (capacity - 1))
     )
     reorder[...] = (from_row == origin).astype(jnp.float32).astype(jnp.bfloat16)
 
@@ -435,11 +441,11 @@
 
     def back_copy(step, distance):
         return pltpu.make_async_remote_copy(
-            src_ref=back_out.at[step, after(distance)],
+            src_ref=back_out.at[step, after[distance]],
             dst_ref=back_in.at[step, me],
             send_sem=back_out_sem.at[step],
             recv_sem=back_in_sem.at[step],
-            device_id=holder(after(distance)),
+            device_id=holder[distance],
             device_id_type=MESH,
         )
 
@@ -497,10 +503,11 @@
         all_back(step).wait_recv()
         mixed = jnp.dot(
             share_ref[...],
-            back_in[step].reshape(packed, span).astype(jnp.float32),
-            precision=lax.Precision.HIGHEST,
+            back_in[step].reshape(packed, span),
             preferred_element_type=jnp.float32,
         )
+        terms = fold * rows
+        mixed = mixed[:terms] + (mixed[terms : 2 * terms] + mixed[2 * terms :])
         for i in range(fold):
             where = slice(step * chunk + i * span, step * chunk + (i + 1) * span)
             out_ref[:, where] = (
@@ -560,7 +567,7 @@
             dma((tensor_ranks - 1,)),
             dma((tensor_ranks - 1,)),
             pltpu.VMEM(resid.shape, f32),
-            pltpu.VMEM((fold * rows, E * PACKED_ROWS), f32),
+            pltpu.VMEM((3 * fold * rows, E * PACKED_ROWS), bf16),
             pltpu.VMEM((E, PACKED_ROWS, width), bf16),
             pltpu.VMEM((2, E, PACKED_ROWS, width), bf16),
             dma(()),

time: 40.8 us -> 40.7 us (level)
  no operation moved by 1% of the time
where the time goes in v5:
time: 40.7 us; the launch traced here: 40.5 us
  Pallas kernels  39.1 us (96%)
  local copies, waits for them, and re-layouts  1.42 us (3%)
    pallas_call x1, Pallas kernels, fused_shards(): pl.pallas_call(functools.partial(fused_kernel, (E, tensor_ranks, capacity...  39.1 us
    unnamed x1, local copies, waits for them, and re-layouts  1.42 us

profile of v5, /device:TPU:0, one launch (start us, length us, event | category | flops | bytes accessed | tf_op | source)
XLA Modules:
  0.0 40.5 jit_solution(13283364648319675439)
XLA Ops:
  0.0 39.1 %shard_map.82 = bf16[8,3072]{1,0:T(8,128)(2,1)} custom-call(bf16[8,3072]{1,0:T(8,128)(2,1)} %resid_hbm.1, bf16[32,3072]{1,0:T(8,128)(2,1)} %attn_hbm.1, f32[1,3072]{1,0:T(1,128)} %bitcast.4, bf16[8,3072]{1,0:T(8,128)(2,1)} %bitcast.3, s32[2,8]{1,0:T(2,128)} %bitcast.5, bf16[3072,4096]{1,0:T(8,128)(2,1)} %gate_hbm.1, bf16[3072,4096]{1,0:T(8,128)(2,1)} %up_hbm.1, ...), custom_call_target="tpu_custom_call" | custom-call | flops 4831838208 | bytes 75497472 | tf_op jit(solution)/shard_map/pallas_call | solution.py:549
  39.1 1.4 %copy.10 = bf16[8,3072]{1,0:T(8,128)(2,1)} copy(bf16[8,3072]{1,0:T(8,128)(2,1)} %shard_map.82) | data formatting | bytes 98304

commit v6 on v5

--- a/solution.py
+++ b/solution.py
@@ -125,7 +125,7 @@
 LANES = 128
 PACKED_ROWS = 16
 WEIGHT_BYTES = 52 << 20
-VMEM_BYTES = 60 << 20
+VMEM_BYTES = 61 << 20
 
 
 def log(power):
@@ -168,6 +168,8 @@
     select,
     reorder,
     tokens,
+    gate_sum,
+    up_sum,
     activated,
     partial_ref,
     half_out,
@@ -182,9 +184,13 @@
     experts, tensor_ranks, capacity, hidden_slots, down_slots = sizes
     rows, features = resid.shape
     fold = PACKED_ROWS // capacity
-    width = features // fold
-    hidden_step = hidden_weights.shape[3]
-    hidden_steps = gate_hbm.shape[1] // hidden_step
+    parts = slots_out.shape[0]
+    part_features = features // parts
+    width = part_features // fold
+    hidden_units = gate_hbm.shape[1]
+    hidden_step = hidden_weights.shape[2]
+    hidden_steps = features // hidden_step
+    part_steps = hidden_steps // parts
     down_step = down_weights.shape[2]
     chunks, _, _, chunk = partial_ref.shape
     chunk_steps = chunk // down_step
@@ -226,10 +232,10 @@
         pl.semaphore_signal(barrier, inc=1, device_id=peer, device_id_type=MESH)
 
     def hidden_copies(step, slot):
-        columns = pl.ds(pl.multiple_of(step * hidden_step, hidden_step), hidden_step)
+        inputs = pl.ds(step * hidden_step, hidden_step)
         return [
             pltpu.make_async_copy(
-                source.at[:, columns], hidden_weights.at[slot, i], hidden_sem.at[slot, i]
+                source.at[inputs], hidden_weights.at[slot, i], hidden_sem.at[slot, i]
             )
             for i, source in enumerate((gate_hbm, up_hbm))
         ]
@@ -313,46 +319,57 @@
     mean_square = jnp.sum(hidden_wide * hidden_wide, axis=1, keepdims=True) / features
     normed_wide = hidden_wide * lax.rsqrt(mean_square + EPSILON) * gain[...]
     normed = normed_wide.astype(jnp.bfloat16)
-    folded = jnp.concatenate(
-        [normed_wide[:, i * width : (i + 1) * width] for i in range(fold)], axis=0
-    ).astype(jnp.bfloat16)
-    outgoing = jnp.dot(placement, folded, preferred_element_type=jnp.float32)
-    slots_out[...] = outgoing.astype(jnp.bfloat16).reshape(experts, PACKED_ROWS, width)
-
-    def slot_copy(step):
+
+    def slot_copy(part, step):
         return pltpu.make_async_remote_copy(
-            src_ref=slots_out.at[after[step]],
-            dst_ref=slots_in.at[core, me],
-            send_sem=slots_out_sem,
-            recv_sem=slots_in_sem,
+            src_ref=slots_out.at[part, after[step]],
+            dst_ref=slots_in.at[part, core, me],
+            send_sem=slots_out_sem.at[part],
+            recv_sem=slots_in_sem.at[part],
             device_id=holder[step],
             device_id_type=MESH,
         )
 
     others = pl.ds(0, experts - 1)
-    all_slots = pltpu.make_async_remote_copy(
-        src_ref=slots_out.at[others],
-        dst_ref=slots_in.at[core, others],
-        send_sem=slots_out_sem,
-        recv_sem=slots_in_sem,
-        device_id=sibling,
-        device_id_type=MESH,
-    )
-    pass_copy = pltpu.make_async_remote_copy(
-        src_ref=slots_in.at[core],
-        dst_ref=slots_in.at[core],
-        send_sem=pass_out_sem,
-        recv_sem=pass_in_sem,
-        device_id=sibling,
-        device_id_type=MESH,
-    )
-    for step in sorted(range(1, experts), key=lambda step: abs(2 * step - experts - 1)):
-        slot_copy(step).start()
+
+    def all_slots(part):
+        return pltpu.make_async_remote_copy(
+            src_ref=slots_out.at[part, others],
+            dst_ref=slots_in.at[part, core, others],
+            send_sem=slots_out_sem.at[part],
+            recv_sem=slots_in_sem.at[part],
+            device_id=sibling,
+            device_id_type=MESH,
+        )
+
+    def pass_copy(part):
+        return pltpu.make_async_remote_copy(
+            src_ref=slots_in.at[part, core],
+            dst_ref=slots_in.at[part, core],
+            send_sem=pass_out_sem.at[part],
+            recv_sem=pass_in_sem.at[part],
+            device_id=sibling,
+            device_id_type=MESH,
+        )
+
+    for part in range(parts):
+        start = part * part_features
+        folded = jnp.concatenate(
+            [
+                normed_wide[:, start + i * width : start + (i + 1) * width]
+                for i in range(fold)
+            ],
+            axis=0,
+        ).astype(jnp.bfloat16)
+        outgoing = jnp.dot(placement, folded, preferred_element_type=jnp.float32)
+        slots_out[part] = outgoing.astype(jnp.bfloat16).reshape(experts, PACKED_ROWS, width)
+        for step in sorted(range(1, experts), key=lambda step: abs(2 * step - experts - 1)):
+            slot_copy(part, step).start()
+        slots_in[part, core, me] = slots_out[part, me]
     for step in range(2, hidden_slots):
         start_hidden(step)
     for step in range(down_slots):
         down_copy(step, step).start()
-    slots_in[core, me] = slots_out[me]
 
     logits = lax.dot_general(
         normed, router[...], (((1,), (1,)), ((), ())), preferred_element_type=jnp.float32
@@ -390,44 +407,43 @@
     )
     reorder[...] = (from_row == origin).astype(jnp.float32).astype(jnp.bfloat16)
 
-    all_slots.wait_recv()
-    pass_copy.start()
-    pass_copy.wait_recv()
-    arrived = slots_in[...].reshape(sources * PACKED_ROWS, width)
-    for i in range(fold):
-        tokens[:, i * width : (i + 1) * width] = jnp.dot(
-            select[i], arrived, preferred_element_type=jnp.float32
-        ).astype(jnp.bfloat16)
+    def receive(part):
+        all_slots(part).wait_recv()
+        pass_copy(part).start()
+        pass_copy(part).wait_recv()
+        arrived = slots_in[part].reshape(sources * PACKED_ROWS, width)
+        for i in range(fold):
+            place, column = divmod(i * width, hidden_step)
+            tokens[part * part_steps + place, :, column : column + width] = jnp.dot(
+                select[i], arrived, preferred_element_type=jnp.float32
+            ).astype(jnp.bfloat16)
 
     tile = fold * LANES
-
-    def hidden_body(step, carry):
+    for step in range(hidden_steps):
         slot = step % hidden_slots
+        if step % part_steps == 0:
+            receive(step // part_steps)
         for copy in hidden_copies(step, slot):
             copy.wait()
-        for start in range(0, hidden_step, tile):
-            gate_value = jnp.dot(
-                tokens[...],
-                hidden_weights[slot, 0, :, start : start + tile],
-                preferred_element_type=jnp.float32,
-            )
-            up_value = jnp.dot(
-                tokens[...],
-                hidden_weights[slot, 1, :, start : start + tile],
-                preferred_element_type=jnp.float32,
-            )
-            value = gate_value / (1.0 + jnp.exp(-gate_value)) * up_value
-            where = pl.ds(pl.multiple_of(step * hidden_step + start, tile), tile)
-            activated[:, where] = value.astype(jnp.bfloat16)
-
-        @pl.when(step + hidden_slots < hidden_steps)
-        def _():
+        for start in range(0, hidden_units, tile):
+            where = slice(start, start + tile)
+            values = []
+            for i, total in enumerate((gate_sum, up_sum)):
+                value = jnp.dot(
+                    tokens[step],
+                    hidden_weights[slot, i, :, where],
+                    preferred_element_type=jnp.float32,
+                )
+                values.append(value if step == 0 else total[:, where] + value)
+            if step < hidden_steps - 1:
+                gate_sum[:, where], up_sum[:, where] = values
+            else:
+                gate_value, up_value = values
+                value = gate_value / (1.0 + jnp.exp(-gate_value)) * up_value
+                activated[:, where] = value.astype(jnp.bfloat16)
+        if step + hidden_slots < hidden_steps:
             for copy in hidden_copies(step + hidden_slots, slot):
                 copy.start()
-
-        return carry
-
-    lax.fori_loop(0, hidden_steps, hidden_body, 0)
 
     def half_copy(step):
         return pltpu.make_async_remote_copy(
@@ -520,8 +536,11 @@
     for step in range(max(0, chunks - 2), chunks):
         combine(step)
 
-    for copy in attn_copies + [all_slots, pass_copy]:
+    for copy in attn_copies:
         copy.wait_send()
+    for part in range(parts):
+        all_slots(part).wait_send()
+        pass_copy(part).wait_send()
     for step in range(chunks):
         half_copy(step).wait_send()
         all_back(step).wait_send()
@@ -532,15 +551,16 @@
     rows, features = resid.shape
     capacity = rows // 2
     fold = PACKED_ROWS // capacity
-    width = features // fold
     hidden_units = w_gate.shape[1]
+    parts = 2
+    width = features // parts // fold
     step = fold * LANES
-    hidden_step = 2 * step if hidden_units % (2 * step) == 0 else step
-    hidden_steps, down_steps = hidden_units // hidden_step, features // step
+    hidden_step = 2 * width
+    hidden_steps, down_steps = features // hidden_step, features // step
     down_slots = min(down_steps, 4)
     chunk = 2 * step if down_steps % 2 == 0 else step
     chunks = features // chunk
-    hidden_bytes, down_bytes = 4 * features * hidden_step, 2 * hidden_units * step
+    hidden_bytes, down_bytes = 4 * hidden_units * hidden_step, 2 * hidden_units * step
     hidden_slots = min(hidden_steps, (WEIGHT_BYTES - down_slots * down_bytes) // hidden_bytes)
     dma = pltpu.SemaphoreType.DMA
     bf16, f32 = jnp.bfloat16, jnp.float32
@@ -558,7 +578,7 @@
             pltpu.VMEM(w_router.shape[::-1], bf16),
             pltpu.VMEM(routes.shape[::-1], jnp.int32),
             dma((5,)),
-            pltpu.VMEM((hidden_slots, 2, features, hidden_step), bf16),
+            pltpu.VMEM((hidden_slots, 2, hidden_step, hidden_units), bf16),
             dma((hidden_slots, 2)),
             pltpu.VMEM((down_slots, hidden_units, step), bf16),
             dma((down_slots,)),
@@ -568,15 +588,17 @@
             dma((tensor_ranks - 1,)),
             pltpu.VMEM(resid.shape, f32),
             pltpu.VMEM((3 * fold * rows, E * PACKED_ROWS), bf16),
-            pltpu.VMEM((E, PACKED_ROWS, width), bf16),
-            pltpu.VMEM((2, E, PACKED_ROWS, width), bf16),
-            dma(()),
-            dma(()),
-            dma(()),
-            dma(()),
+            pltpu.VMEM((parts, E, PACKED_ROWS, width), bf16),
+            pltpu.VMEM((parts, 2, E, PACKED_ROWS, width), bf16),
+            dma((parts,)),
+            dma((parts,)),
+            dma((parts,)),
+            dma((parts,)),
             pltpu.VMEM((fold, 2 * half_rows, 2 * E * PACKED_ROWS), bf16),
             pltpu.VMEM((E * PACKED_ROWS, E * PACKED_ROWS), bf16),
-            pltpu.VMEM((2 * half_rows, features), bf16),
+            pltpu.VMEM((hidden_steps, 2 * half_rows, hidden_step), bf16),
+            pltpu.VMEM((2 * half_rows, hidden_units), f32),
+            pltpu.VMEM((2 * half_rows, hidden_units), f32),
             pltpu.VMEM((2 * half_rows, hidden_units), bf16),
             pltpu.VMEM((chunks, 2, half_rows, chunk), f32),
             pltpu.VMEM((chunks, half_rows, chunk), bf16),

time: 40.7 us -> 40.1 us (0.985)
  Pallas kernels: 39.1 us -> 38.5 us
    pallas_call x1, Pallas kernels: 39.1 us -> 38.5 us  [fused_shards(): pl.pallas_call(functools.partial(fused_kernel, (E, tensor_ranks, capacity...]
where the time goes in v6:
time: 40.1 us; the launch traced here: 40 us
  Pallas kernels  38.5 us (96%)
  local copies, waits for them, and re-layouts  1.42 us (4%)
    pallas_call x1, Pallas kernels, fused_shards(): pl.pallas_call(functools.partial(fused_kernel, (E, tensor_ranks, capacity...  38.5 us
    unnamed x1, local copies, waits for them, and re-layouts  1.42 us

profile of v6, /device:TPU:0, one launch (start us, length us, event | category | flops | bytes accessed | tf_op | source)
XLA Modules:
  0.0 40.0 jit_solution(781072885595366183)
XLA Ops:
  0.0 38.5 %shard_map.82 = bf16[8,3072]{1,0:T(8,128)(2,1)} custom-call(bf16[8,3072]{1,0:T(8,128)(2,1)} %resid_hbm.1, bf16[32,3072]{1,0:T(8,128)(2,1)} %attn_hbm.1, f32[1,3072]{1,0:T(1,128)} %bitcast.4, bf16[8,3072]{1,0:T(8,128)(2,1)} %bitcast.3, s32[2,8]{1,0:T(2,128)} %bitcast.5, bf16[3072,4096]{1,0:T(8,128)(2,1)} %gate_hbm.1, bf16[3072,4096]{1,0:T(8,128)(2,1)} %up_hbm.1, ...), custom_call_target="tpu_custom_call" | custom-call | flops 4831838208 | bytes 75497472 | tf_op jit(solution)/shard_map/pallas_call | solution.py:569
  38.5 1.4 %copy.10 = bf16[8,3072]{1,0:T(8,128)(2,1)} copy(bf16[8,3072]{1,0:T(8,128)(2,1)} %shard_map.82) | data formatting | bytes 98304

commit v7 on v6

--- a/solution.py
+++ b/solution.py
@@ -250,7 +250,8 @@
         for copy in hidden_copies(step, step):
             copy.start()
 
-    start_hidden(0)
+    for step in range(hidden_slots):
+        start_hidden(step)
     small[0].wait()
     terms = attn[...].astype(jnp.float32)
     half = features // 2
@@ -275,8 +276,6 @@
     attn_copies = [attn_copy(step) for step in range(1, tensor_ranks)]
     for copy in attn_copies:
         copy.start()
-    for step in range(1, min(2, hidden_slots)):
-        start_hidden(step)
     for copy in small[1:]:
         copy.wait()
     diagonal = lax.broadcasted_iota(jnp.int32, (rows, rows), 0) == lax.broadcasted_iota(
@@ -366,8 +365,6 @@
         for step in sorted(range(1, experts), key=lambda step: abs(2 * step - experts - 1)):
             slot_copy(part, step).start()
         slots_in[part, core, me] = slots_out[part, me]
-    for step in range(2, hidden_slots):
-        start_hidden(step)
     for step in range(down_slots):
         down_copy(step, step).start()
 

time: 40.1 us -> 40.2 us (level)
  no operation moved by 1% of the time
where the time goes in v7:
time: 40.2 us; the launch traced here: 40 us
  Pallas kernels  38.6 us (96%)
  local copies, waits for them, and re-layouts  1.42 us (4%)
    pallas_call x1, Pallas kernels, fused_shards(): pl.pallas_call(functools.partial(fused_kernel, (E, tensor_ranks, capacity...  38.6 us
    unnamed x1, local copies, waits for them, and re-layouts  1.42 us

profile of v7, /device:TPU:0, one launch (start us, length us, event | category | flops | bytes accessed | tf_op | source)
XLA Modules:
  0.0 40.0 jit_solution(9619092791424272412)
XLA Ops:
  0.0 38.6 %shard_map.82 = bf16[8,3072]{1,0:T(8,128)(2,1)} custom-call(bf16[8,3072]{1,0:T(8,128)(2,1)} %resid_hbm.1, bf16[32,3072]{1,0:T(8,128)(2,1)} %attn_hbm.1, f32[1,3072]{1,0:T(1,128)} %bitcast.4, bf16[8,3072]{1,0:T(8,128)(2,1)} %bitcast.3, s32[2,8]{1,0:T(2,128)} %bitcast.5, bf16[3072,4096]{1,0:T(8,128)(2,1)} %gate_hbm.1, bf16[3072,4096]{1,0:T(8,128)(2,1)} %up_hbm.1, ...), custom_call_target="tpu_custom_call" | custom-call | flops 4831838208 | bytes 75497472 | tf_op jit(solution)/shard_map/pallas_call | solution.py:566
  38.6 1.4 %copy.10 = bf16[8,3072]{1,0:T(8,128)(2,1)} copy(bf16[8,3072]{1,0:T(8,128)(2,1)} %shard_map.82) | data formatting | bytes 98304
